TPU v7x, 32 devices: a whole 2x2x4 slice. The times are simulated.
32 devices in a mesh: rep: 8 (over z, x), fsdp: 4 (over y, core).
Axes of the slice: x: 2, y: 2, z: 4, core: 2. Of those that a mesh axis runs over, the one named last changes fastest.
Arguments:
- tokens: bfloat16 [32768, 1024], P(('rep', 'fsdp')), may hold values from -6 to 6
- norm_w: bfloat16 [1024], P('fsdp'), may hold values from 0.099609375 to 1.8984375
- in_w: bfloat16 [1024, 4384], P('fsdp'), may hold values from -0.1875 to 0.1875
- conv_w: bfloat16 [4, 2304], P(None, 'fsdp'), may hold values from -3 to 3
- conv_b: bfloat16 [2304], P('fsdp'), may hold values from -0.5 to 0.5
- dt_bias: bfloat16 [32], P('fsdp'), may hold values from -2 to 0.5
- a_log: bfloat16 [32], P('fsdp'), may hold values from -8 to 0.5
- d_skip: bfloat16 [32], P('fsdp'), may hold values from 0.5 to 1.5
- gnorm_w: bfloat16 [2048], P('fsdp'), may hold values from 0.099609375 to 1.8984375
- out_w: bfloat16 [2048, 1024], P('fsdp'), may hold values from -0.125 to 0.125
- first_length: int32 [8], P('rep'), may hold values from 1024 to 3072, as said below
- cotangent: bfloat16 [32768, 1024], P(('rep', 'fsdp')), may hold values from -6 to 6
Outputs:
- output: bfloat16 [32768, 1024], P(('rep', 'fsdp'))
- d_tokens: float32 [32768, 1024], P(('rep', 'fsdp'))
- d_norm_w: float32 [1024], P('fsdp')
- d_in_w: float32 [1024, 4384], P('fsdp')
- d_conv_w: float32 [4, 2304], P(None, 'fsdp')
- d_conv_b: float32 [2304], P('fsdp')
- d_dt_bias: float32 [32], P('fsdp')
- d_a_log: float32 [32], P('fsdp')
- d_d_skip: float32 [32], P('fsdp')
- d_gnorm_w: float32 [2048], P('fsdp')
- d_out_w: float32 [2048, 1024], P('fsdp')
Inputs may be any that keep to these rules, and one draw needn't show every extreme that they name: The second sequence of group g has 4096 - first_length[g] tokens; some group has each end of the range.
All inputs are finite; a program needn't handle non-finite values.
Results may differ from a plain program's by a relative error of at most 0.0061.
Values may be sent and summed in bfloat16 or wider, within the bound.
A program may use at most 256 MiB of HBM per device.

v0:
```python
import math

import jax
import jax.numpy as jnp
from jax import lax
from jax.sharding import PartitionSpec as P

H = 32
P_SIZE = 64
N = 128
K = 4
Q = 256
E = 2048


highest = lax.Precision.HIGHEST
epsilon = 1e-05


def shifted(x, axis, by):
    peers = lax.axis_size(axis)
    pairs = [(i, i + by) for i in range(peers) if 0 <= i + by < peers]
    return lax.ppermute(x, axis, pairs)


def prefix(part, axis, combine, identity, reverse):
    count = lax.axis_size(axis)
    place = lax.axis_index(axis)
    ahead = count - 1 - place if reverse else place
    gathered = jax.tree.map(lambda a: lax.all_gather(a, axis), part)
    state = jax.tree.map(lambda a, e: jnp.zeros_like(a) + jnp.asarray(e, a.dtype), part, identity)

    def one(step, state):
        source = count - 1 - step if reverse else step
        return combine(
            state, jax.tree.map(lambda a: lax.dynamic_index_in_dim(a, source, 0, False), gathered)
        )

    return lax.fori_loop(0, ahead, one, state)


def rms_scale(values):
    return values * lax.rsqrt(jnp.mean(values * values, axis=-1, keepdims=True) + epsilon)


def prenorm(values, gain):
    return rms_scale(values) * gain[None, :]


def gate_norm(result, z_part, gain):
    return rms_scale(result * jax.nn.silu(z_part)) * gain


def convolve(full, conv_w, conv_b, places, starts):
    taps = conv_w.shape[0]
    length = places.shape[0]
    total = jnp.zeros((length, full.shape[1]), jnp.float32) + conv_b[None, :]
    for index in range(taps):
        source = places - (taps - 1) + index
        valid = (source >= starts).astype(jnp.float32)
        total = total + full[index : index + length] * conv_w[index][None, :] * valid[:, None]
    return jax.nn.silu(total)


def span_step(state, pieces):
    xs_part, delta, bmat, cmat, decay, segment, seg_prev = pieces
    cumul = jnp.cumsum(decay, axis=0)
    count = segment.shape[0]
    spots = jnp.arange(count, dtype=jnp.int32)
    causal = (spots[:, None] >= spots[None, :]) & (segment[:, None] == segment[None, :])
    spread = cumul.T[:, :, None] - cumul.T[:, None, :]
    weights = jnp.exp(jnp.where(causal[None], spread, jnp.zeros_like(spread))) * causal[
        None
    ].astype(jnp.float32)
    inner = jnp.dot(cmat, bmat.T, precision=highest, preferred_element_type=jnp.float32)
    mixing = weights * inner[None] * delta.T[:, None, :]
    intra = jnp.einsum("hts,shp->thp", mixing, xs_part, precision=highest)
    carried = (segment == seg_prev).astype(jnp.float32)
    entry = jnp.exp(cumul) * carried[:, None]
    from_state = jnp.einsum("tn,hpn->thp", cmat, state, precision=highest) * entry[:, :, None]
    last_seg = segment[-1]
    tail = (
        jnp.exp(cumul[-1][None, :] - cumul)
        * (segment == last_seg).astype(jnp.float32)[:, None]
        * delta
    )
    keep_old = jnp.exp(cumul[-1]) * (last_seg == seg_prev).astype(jnp.float32)
    new_state = state * keep_old[:, None, None] + jnp.einsum(
        "sh,shp,sn->hpn", tail, xs_part, bmat, precision=highest
    )
    return (new_state, intra + from_state)


def scan_spans(xs_all, delta, bmat, cmat, decay, segment, seg_before):
    count = xs_all.shape[0] // Q

    def split_up(values):
        return values.reshape((count, Q) + values.shape[1:])

    seg_blocks = split_up(segment)
    seg_prev = jnp.concatenate([jnp.reshape(seg_before, (1,)), seg_blocks[:-1, -1]])
    zero_state = jnp.zeros((H, P_SIZE, N), jnp.float32)
    final, pieces = lax.scan(
        jax.checkpoint(span_step),
        zero_state,
        (
            split_up(xs_all),
            split_up(delta),
            split_up(bmat),
            split_up(cmat),
            split_up(decay),
            seg_blocks,
            seg_prev,
        ),
    )
    return (final, pieces.reshape(xs_all.shape))


def ssm_inputs(
    proj, rim_rows, conv_w, conv_b, dt_bias, a_log, d_skip, places, starts, segment, seg_before
):
    length = proj.shape[0]
    xbc = proj[:, E : 2 * E + 2 * N]
    full = jnp.concatenate([rim_rows, xbc], axis=0)
    mixed = convolve(full, conv_w, conv_b, places, starts)
    xs_all = mixed[:, :E].reshape(length, H, P_SIZE)
    bmat = mixed[:, E : E + N]
    cmat = mixed[:, E + N :]
    delta = jax.nn.softplus(proj[:, 2 * E + 2 * N :] + dt_bias[None, :])
    decay = -jnp.exp(a_log)[None, :] * delta
    final, result = scan_spans(xs_all, delta, bmat, cmat, decay, segment, seg_before)
    result = result + d_skip[None, :, None] * xs_all
    return (result, cmat, decay, final)


def compose(earlier, later):
    return (earlier[0] * later[0], later[0][:, None, None] * earlier[1] + later[1])


def owner_major(grad, axis_num, owners):
    return jnp.moveaxis(grad, axis_num, 0).reshape((owners, -1))


def unpack(flat, shapes, axes):
    pieces = []
    offset = 0
    for shape, axis_num in zip(shapes, axes):
        moved = (shape[axis_num],) + tuple(
            (extent for place, extent in enumerate(shape) if place != axis_num)
        )
        amount = math.prod(moved)
        piece = flat[offset : offset + amount].reshape(moved)
        pieces.append(jnp.moveaxis(piece, 0, axis_num))
        offset = offset + amount
    return pieces


def body(
    tokens,
    norm_w,
    in_w,
    conv_w,
    conv_b,
    dt_bias,
    a_log,
    d_skip,
    gnorm_w,
    out_w,
    first_length,
    cotangent,
):
    shards = (norm_w, in_w, conv_w, conv_b, dt_bias, a_log, d_skip, gnorm_w, out_w)
    shard_axes = (0, 0, 1, 0, 0, 0, 0, 0, 0)
    whole = (
        lax.all_gather(norm_w, "fsdp", axis=0, tiled=True),
        lax.all_gather(in_w, "fsdp", axis=0, tiled=True),
        lax.all_gather(conv_w, "fsdp", axis=1, tiled=True),
        lax.all_gather(conv_b, "fsdp", axis=0, tiled=True),
        lax.all_gather(dt_bias, "fsdp", axis=0, tiled=True),
        lax.all_gather(a_log, "fsdp", axis=0, tiled=True),
        lax.all_gather(d_skip, "fsdp", axis=0, tiled=True),
        lax.all_gather(gnorm_w, "fsdp", axis=0, tiled=True),
        lax.all_gather(out_w, "fsdp", axis=0, tiled=True),
    )
    g_norm, g_in, g_conv, g_bias, g_dt, g_alog, g_skip, g_gnorm, g_out = whole
    norm32 = g_norm.astype(jnp.float32)
    conv32 = g_conv.astype(jnp.float32)
    bias32 = g_bias.astype(jnp.float32)
    dt32 = g_dt.astype(jnp.float32)
    alog32 = g_alog.astype(jnp.float32)
    skip32 = g_skip.astype(jnp.float32)
    gnorm32 = g_gnorm.astype(jnp.float32)
    length = tokens.shape[0]
    first_place = lax.axis_index("fsdp") * length
    places = first_place + jnp.arange(length, dtype=jnp.int32)
    boundary = first_length[0]
    starts = jnp.where(places >= boundary, boundary, jnp.zeros_like(boundary))
    segment = (places >= boundary).astype(jnp.int32)
    seg_before = (first_place - 1 >= boundary).astype(jnp.int32)
    keep_mask = (segment == seg_before).astype(jnp.float32)
    inputs_f = tokens.astype(jnp.float32)
    normed32, pull_norm = jax.vjp(prenorm, inputs_f, norm32)
    normed = normed32.astype(jnp.bfloat16)
    proj = jnp.dot(normed, g_in, preferred_element_type=jnp.float32)
    xbc_tail = proj[length - (K - 1) :, E : 2 * E + 2 * N]
    rim_rows = shifted(xbc_tail, "fsdp", 1)

    def front(proj_in, rim_in, conv_in, bias_in, dt_in, alog_in, skip_in):
        result, cmat, decay, final = ssm_inputs(
            proj_in,
            rim_in,
            conv_in,
            bias_in,
            dt_in,
            alog_in,
            skip_in,
            places,
            starts,
            segment,
            seg_before,
        )
        cumdev = jnp.cumsum(decay, axis=0)
        total = jnp.exp(cumdev[-1]) * keep_mask[-1]
        return (result, cmat, cumdev, final, total)

    (result, cmat, cumdev, final, total), pull_front = jax.vjp(
        front, proj, rim_rows, conv32, bias32, dt32, alog32, skip32
    )
    identity = (jnp.ones((H,), jnp.float32), jnp.zeros((H, P_SIZE, N), jnp.float32))
    inflow = prefix((total, final), "fsdp", compose, identity, False)
    state_in = inflow[1]

    def back_half(result_in, cmat_in, cumdev_in, z_part, gain, incoming):
        reach = jnp.exp(cumdev_in) * keep_mask[:, None]
        added = jnp.einsum("tn,hpn->thp", cmat_in, incoming, precision=highest) * reach[:, :, None]
        return gate_norm((result_in + added).reshape(length, E), z_part, gain[None, :])

    gated32, pull_back = jax.vjp(back_half, result, cmat, cumdev, proj[:, :E], gnorm32, state_in)
    gated = gated32.astype(jnp.bfloat16)
    output = (inputs_f + jnp.dot(gated, g_out, preferred_element_type=jnp.float32)).astype(
        jnp.bfloat16
    )
    w_in, w_out = (
        lax.all_gather(in_w, "fsdp", axis=0, tiled=True),
        lax.all_gather(out_w, "fsdp", axis=0, tiled=True),
    )
    d_out_w = jnp.dot(gated.T, cotangent, preferred_element_type=jnp.float32)
    d_gated = jnp.dot(cotangent, w_out.T, preferred_element_type=jnp.float32)
    d_result, d_cmat, d_cumdev, d_zpart, d_gnorm, state_grad = pull_back(d_gated)
    behind = prefix((total, state_grad), "fsdp", compose, identity, True)
    after = behind[1]
    d_total = jnp.sum(after * state_in, axis=(1, 2))
    d_proj, d_rim, d_conv, d_bias, d_dt, d_alog, d_skip = pull_front(
        (d_result, d_cmat, d_cumdev, after, d_total)
    )
    d_proj = d_proj.at[:, :E].add(d_zpart)
    d_tail = shifted(d_rim, "fsdp", -1)
    d_proj = d_proj.at[length - (K - 1) :, E : 2 * E + 2 * N].add(d_tail)
    d_proj_low = d_proj.astype(jnp.bfloat16)
    d_in_w = jnp.dot(normed.T, d_proj_low, preferred_element_type=jnp.float32)
    d_normed = jnp.dot(d_proj_low, w_in.T, preferred_element_type=jnp.float32)
    d_rows, d_norm = pull_norm(d_normed)
    d_tokens = cotangent.astype(jnp.float32) + d_rows
    owners = lax.axis_size("fsdp")
    partials = (d_norm, d_in_w, d_conv, d_bias, d_dt, d_alog, d_skip, d_gnorm, d_out_w)
    stacked = jnp.concatenate(
        [owner_major(grad, axis_num, owners) for grad, axis_num in zip(partials, shard_axes)],
        axis=1,
    )
    mine = lax.psum_scatter(stacked, "fsdp", scatter_dimension=0, tiled=True)
    summed = lax.psum(mine[0], "rep")
    grads = unpack(summed, [value.shape for value in shards], shard_axes)
    return (
        output,
        d_tokens,
        grads[0],
        grads[1],
        grads[2],
        grads[3],
        grads[4],
        grads[5],
        grads[6],
        grads[7],
        grads[8],
    )


def solution(mesh):
    in_specs = (
        P(("rep", "fsdp"), None),
        P("fsdp"),
        P("fsdp", None),
        P(None, "fsdp"),
        P("fsdp"),
        P("fsdp"),
        P("fsdp"),
        P("fsdp"),
        P("fsdp"),
        P("fsdp", None),
        P("rep"),
        P(("rep", "fsdp"), None),
    )
    out_specs = (
        P(("rep", "fsdp"), None),
        P(("rep", "fsdp"), None),
        P("fsdp"),
        P("fsdp", None),
        P(None, "fsdp"),
        P("fsdp"),
        P("fsdp"),
        P("fsdp"),
        P("fsdp"),
        P("fsdp"),
        P("fsdp", None),
    )
    return jax.shard_map(body, mesh=mesh, in_specs=in_specs, out_specs=out_specs, check_vma=False)
```

profile of v0, /device:TPU:0, one launch (start us, length us, event | category | flops | bytes accessed | tf_op | source)
XLA Modules:
  0.0 2377.1 jit_solution(7133981507890704654)
XLA Ops:
  20.7 8.4 all-reduce.21
  39.8 35.7 %all-gather.11.cloned.1.call-done = bf16[1024,4384]{0,1:T(8,128)(2,1)} async-done(((bf16[256,4384]{0,1:T(8,128)(2,1)}), bf16[1024,4384]{0,1:T(8,128)(2,1)}) %all-gather.11.cloned.1.call-update) | async-done | bytes 8978448 | tf_op jit(solution)/shard_map/all_gather | solution.py:176
  75.5 13.1 fusion.132
  98.9 9.3 slice.255
  110.1 24.0 %fusion.100 = (f32[1024,2304]{0,1:T(8,128)S(1)}, f32[1024,2304]{0,1:T(8,128)}) fusion(f32[1024]{0:T(1024)S(1)} %get-tuple-element.1044, f32[1024,2304]{0,1:T(8,128)} %slice.255, f32[2304]{0:T(1024)S(1)} %get-tuple-element.911, f32[1024]{0:T(1024)S(1)} %get-tuple-element.1043, f32[2304]{0:T(1024)S(1)} %get-tuple-element.912, f32[3,2304]{0,1:T(8,128)S(1)} %copy.341, ...), kind=kLoop, calls=%fused_computation.168 | loop fusion | flops 44826624 | bytes 28401664 | tf_op jit(solution)/shard_map/jvp(jit(silu))/mul | solution.py:62
  140.3 10.5 reshape.678
  150.9 8.3 copy.345
  166.5 319.3 %while.70 = (s32[]{:T(128)}, f32[32,64,128]{2,1,0:T(8,128)S(1)}, f32[4,256,32,64]{1,0,3,2:T(4,128)}, f32[4,32,64,128]{3,2,1,0:T(8,128)}, f32[4,256,32]{1,2,0:T(8...) while((s32[]{:T(128)}, f32[32,64,128]{2,1,0:T(8,128)S(1)}, ...), condition=%wide.region_4.5_spmd.clone, body=%wide.region_1.4_spmd.clone.sunk | while | flops 3336610816 | bytes 26490496 | solution.py:103
  172.5 12.0 fusion.264
  200.6 45.8 %dynamic_update_slice.74 = f32[4,256,32,64]{1,0,3,2:T(4,128)} dynamic-update-slice(f32[4,256,32,64]{1,0,3,2:T(4,128)} %get-tuple-element.1364, f32[1,256,32,64]{1,0,3,2:T(1,128)} %copy.524, s32[]{:T(128)S(6)} %copy.540, s32[]{:T(128)} %constant.235.clone.1..sunk.3, s32[]{:T(128)} %constant.235.clone.1..sunk.3, s32[]{:T(128)} %constant.235.clone.1..sunk.3) | dynamic-update-slice | bytes 4194308 | tf_op jit(solution)/shard_map/jvp()/while/body/jit(dynamic_update_index_in_dim)/dynamic_update_slice | solution.py:103
  252.2 12.0 fusion.264
  280.4 45.8 %dynamic_update_slice.74 = f32[4,256,32,64]{1,0,3,2:T(4,128)} dynamic-update-slice(f32[4,256,32,64]{1,0,3,2:T(4,128)} %get-tuple-element.1364, f32[1,256,32,64]{1,0,3,2:T(1,128)} %copy.524, s32[]{:T(128)S(6)} %copy.540, s32[]{:T(128)} %constant.235.clone.1..sunk.3, s32[]{:T(128)} %constant.235.clone.1..sunk.3, s32[]{:T(128)} %constant.235.clone.1..sunk.3) | dynamic-update-slice | bytes 4194308 | tf_op jit(solution)/shard_map/jvp()/while/body/jit(dynamic_update_index_in_dim)/dynamic_update_slice | solution.py:103
  332.0 12.0 fusion.264
  360.2 45.8 %dynamic_update_slice.74 = f32[4,256,32,64]{1,0,3,2:T(4,128)} dynamic-update-slice(f32[4,256,32,64]{1,0,3,2:T(4,128)} %get-tuple-element.1364, f32[1,256,32,64]{1,0,3,2:T(1,128)} %copy.524, s32[]{:T(128)S(6)} %copy.540, s32[]{:T(128)} %constant.235.clone.1..sunk.3, s32[]{:T(128)} %constant.235.clone.1..sunk.3, s32[]{:T(128)} %constant.235.clone.1..sunk.3) | dynamic-update-slice | bytes 4194308 | tf_op jit(solution)/shard_map/jvp()/while/body/jit(dynamic_update_index_in_dim)/dynamic_update_slice | solution.py:103
  411.8 12.0 fusion.264
  440.0 45.8 %dynamic_update_slice.74 = f32[4,256,32,64]{1,0,3,2:T(4,128)} dynamic-update-slice(f32[4,256,32,64]{1,0,3,2:T(4,128)} %get-tuple-element.1364, f32[1,256,32,64]{1,0,3,2:T(1,128)} %copy.524, s32[]{:T(128)S(6)} %copy.540, s32[]{:T(128)} %constant.235.clone.1..sunk.3, s32[]{:T(128)} %constant.235.clone.1..sunk.3, s32[]{:T(128)} %constant.235.clone.1..sunk.3) | dynamic-update-slice | bytes 4194308 | tf_op jit(solution)/shard_map/jvp()/while/body/jit(dynamic_update_index_in_dim)/dynamic_update_slice | solution.py:103
  493.8 9.0 reduce-window.74
  509.3 10.8 reshape.681
  521.7 8.5 fusion.135
  530.2 10.7 multiply_add_fusion.2
  540.9 10.2 multiply_reduce_fusion.13
  551.1 6.5 all-gather.13.cloned.1.call-done
  557.6 14.1 multiply_reduce_fusion.9
  571.8 21.5 multiply_reduce_fusion.10
  593.3 10.0 fusion.108
  604.7 11.0 reshape.687
  617.1 11.9 fusion.154
  629.1 12.5 reshape.707
  641.5 8.7 multiply_reduce_fusion.11
  664.0 626.0 %while.69 = (s32[]{:T(128)}, f32[32,64,128]{2,1,0:T(8,128)S(1)}, f32[4,256,32,64]{1,0,3,2:T(4,128)}, f32[4,256,32]{2,1,0:T(8,128)}, f32[4,256,128]{2,1,0:T(8,128...) while((s32[]{:T(128)}, f32[32,64,128]{2,1,0:T(8,128)S(1)}, ...), condition=%wide.region_25.26_spmd, body=%wide.region_13.25_spmd.sunk | while | flops 7599981568 | bytes 62832580 | solution.py:103
  708.5 16.1 fusion.246
  757.4 9.5 fusion.249
  770.4 45.8 %dynamic_update_slice.71 = f32[4,256,32,64]{1,0,3,2:T(4,128)} dynamic-update-slice(f32[4,256,32,64]{1,0,3,2:T(4,128)} %get-tuple-element.1465, f32[1,256,32,64]{1,0,3,2:T(1,128)} %copy.516, s32[]{:T(128)S(6)} %sub.252, s32[]{:T(128)} %constant.235.clone.1..sunk.2, s32[]{:T(128)} %constant.235.clone.1..sunk.2, s32[]{:T(128)} %constant.235.clone.1..sunk.2) | dynamic-update-slice | bytes 4194308 | tf_op jit(solution)/shard_map/transpose(jvp())/while/body/jit(dynamic_update_index_in_dim)/dynamic_update_slice | solution.py:103
  858.2 16.1 fusion.246
  907.1 9.5 fusion.249
  920.1 45.8 %dynamic_update_slice.71 = f32[4,256,32,64]{1,0,3,2:T(4,128)} dynamic-update-slice(f32[4,256,32,64]{1,0,3,2:T(4,128)} %get-tuple-element.1465, f32[1,256,32,64]{1,0,3,2:T(1,128)} %copy.516, s32[]{:T(128)S(6)} %sub.252, s32[]{:T(128)} %constant.235.clone.1..sunk.2, s32[]{:T(128)} %constant.235.clone.1..sunk.2, s32[]{:T(128)} %constant.235.clone.1..sunk.2) | dynamic-update-slice | bytes 4194308 | tf_op jit(solution)/shard_map/transpose(jvp())/while/body/jit(dynamic_update_index_in_dim)/dynamic_update_slice | solution.py:103
  1007.9 16.1 fusion.246
  1056.8 9.5 fusion.249
  1069.8 45.8 %dynamic_update_slice.71 = f32[4,256,32,64]{1,0,3,2:T(4,128)} dynamic-update-slice(f32[4,256,32,64]{1,0,3,2:T(4,128)} %get-tuple-element.1465, f32[1,256,32,64]{1,0,3,2:T(1,128)} %copy.516, s32[]{:T(128)S(6)} %sub.252, s32[]{:T(128)} %constant.235.clone.1..sunk.2, s32[]{:T(128)} %constant.235.clone.1..sunk.2, s32[]{:T(128)} %constant.235.clone.1..sunk.2) | dynamic-update-slice | bytes 4194308 | tf_op jit(solution)/shard_map/transpose(jvp())/while/body/jit(dynamic_update_index_in_dim)/dynamic_update_slice | solution.py:103
  1157.6 16.1 fusion.246
  1206.5 9.5 fusion.249
  1219.5 45.8 %dynamic_update_slice.71 = f32[4,256,32,64]{1,0,3,2:T(4,128)} dynamic-update-slice(f32[4,256,32,64]{1,0,3,2:T(4,128)} %get-tuple-element.1465, f32[1,256,32,64]{1,0,3,2:T(1,128)} %copy.516, s32[]{:T(128)S(6)} %sub.252, s32[]{:T(128)} %constant.235.clone.1..sunk.2, s32[]{:T(128)} %constant.235.clone.1..sunk.2, s32[]{:T(128)} %constant.235.clone.1..sunk.2) | dynamic-update-slice | bytes 4194308 | tf_op jit(solution)/shard_map/transpose(jvp())/while/body/jit(dynamic_update_index_in_dim)/dynamic_update_slice | solution.py:103
  1290.1 8.9 copy.451
  1299.4 8.1 fusion.128
  1307.6 10.1 multiply_add_fusion.1
  1319.5 24.0 %fusion.155 = (f32[2304]{0:T(1024)S(1)}, f32[2304]{0:T(1024)S(1)}, f32[2304]{0:T(1024)S(1)}, f32[2304]{0:T(1024)S(1)}, f32[2304]{0:T(1024)S(1)}, /*index=5*/f32[1024,2304]{0,1:T(8,128)}) fusion(f32[1024]{0:T(1024)S(1)} %copy-done.40, f32[1024,4384]{0,1:T(8,128)S(1)} %bitcast.459, f32[1024]{0:T(1024)S(1)} %copy-done.42, f32[1024,2304]{0,1:T(8,128)} %slice.255, ...), kind=kLoop, calls=%fused_computation.282 | loop fusion | flops 63689472 | bytes 47276032 | tf_op jit(solution)/shard_map/transpose(jvp())/reduce_sum | solution.py:57
  1343.5 11.1 multiply_multiply_fusion.5
  1354.6 15.5 pad_add_fusion.1
  1374.5 39.6 %reduce-window.76 = f32[32,8,128]{2,1,0:T(8,128)S(1)} reduce-window(f32[32,8,128]{2,1,0:T(8,128)S(1)} %bitcast.486, f32[]{:T(128)} %constant.236.clone.1), window={size=1x1x128 pad=0_0x0_0x0_127}, to_apply=%region_28.29 | reduce-window | flops 4161536 | bytes 262148 | tf_op jit(solution)/shard_map/reduce-window.8
  1414.5 10.2 split.8
  1427.7 11.1 pad_add_fusion
  1438.9 10.0 fusion.103
  1453.0 7.8 scatter-add.9
  1460.8 19.9 fusion.112
  1480.7 18.0 fusion.117
  1499.3 23.1 reshape.770
  1522.4 22.6 reshape.696
  1545.0 12.9 constant_dynamic-update-slice_fusion.1
  1565.7 43.9 %dynamic-update-slice.17 = f32[4,1650264]{1,0:T(4,128)} dynamic-update-slice(f32[4,1650264]{1,0:T(4,128)} %dynamic-update-slice.16, f32[4,524288]{1,0:T(4,128)} %reshape.707, s32[]{} %constant.327, s32[]{} %constant.335) | dynamic-update-slice | bytes 16777220 | tf_op jit(solution)/shard_map/concatenate | solution.py:266
  1609.7 444.7 %all-reduce.27.cloned.1.call-done = f32[4,1650264]{1,0:T(4,128)} async-done(((f32[4,1650264]{1,0:T(4,128)}), f32[4,1650264]{1,0:T(4,128)}) %all-reduce.27.cloned.1.call-update) | async-done | bytes 26404240
  2054.4 66.8 %dynamic-slice_reduce_fusion = f32[1650264]{0:T(1024)} fusion(f32[4,1650264]{1,0:T(4,128)} %all-reduce.27.cloned.1.call-done, u32[]{:T(128)} %bitcast.89), kind=kLoop, calls=%fused_computation.199 | loop fusion | bytes 13202116 | tf_op jit(solution)/shard_map/squeeze | solution.py:271
  2121.3 10.9 fusion.120
  2134.9 208.4 %all-reduce.25.cloned.1.call-done = f32[1650264]{0:T(1024)} async-done(((f32[1650264]{0:T(1024)}), f32[1650264]{0:T(1024)}) %all-reduce.25.cloned.1.call-update) | async-done | bytes 6601072 | tf_op jit(solution)/shard_map/psum | solution.py:271
  2347.2 6.2 reshape.708
  (620 shorter events, 519.6 us)
Async XLA Ops:
  7.2 68.3 %all-gather.11.cloned.1.call-start = ((), (), s32[]{:S(2)}) async-start(), calls=%async_computation | async-start | bytes 11223040 | tf_op jit(solution)/shard_map/all_gather | solution.py:176
  7.9 513.6 %all-gather.15.cloned.1.call-start = ((), (), s32[]{:S(2)}) async-start(), calls=%async_computation.3 | async-start | bytes 5242880 | tf_op jit(solution)/shard_map/all_gather | solution.py:30
  14.7 60.9 %copy-start.53 = (f32[4,1,256]{2,1,0:T(1,128)}, f32[4,1,256]{2,1,0:T(1,128)S(1)}, u32[]{:S(2)}) copy-start(f32[4,1,256]{2,1,0:T(1,128)S(1)} %convert_element_type.174) | copy-start | bytes 12292
  29.1 59.5 %copy-start.66 = (bf16[32]{0:T(256)(128)(2,1)}, bf16[32]{0:T(256)(128)(2,1)S(1)}, u32[]{:S(2)}) copy-start(bf16[32]{0:T(256)(128)(2,1)S(1)} %get-tuple-element.989) | copy-start | bytes 196
  29.1 68.7 %copy-start.60 = (f32[32]{0:T(128)}, f32[32]{0:T(128)S(1)}, u32[]{:S(2)}) copy-start(f32[32]{0:T(128)S(1)} %convert_element_type.157) | copy-start | bytes 388
  37.5 72.5 %copy-start.37 = (f32[1024]{0:T(1024)}, f32[1024]{0:T(1024)S(1)}, u32[]{:S(2)}) copy-start(f32[1024]{0:T(1024)S(1)} %get-tuple-element.1043) | copy-start | bytes 12292
  37.5 72.5 %copy-start.39 = (f32[1024]{0:T(1024)}, f32[1024]{0:T(1024)S(1)}, u32[]{:S(2)}) copy-start(f32[1024]{0:T(1024)S(1)} %get-tuple-element.1044) | copy-start | bytes 12292
  37.5 72.5 %copy-start.41 = (f32[1024]{0:T(1024)}, f32[1024]{0:T(1024)S(1)}, u32[]{:S(2)}) copy-start(f32[1024]{0:T(1024)S(1)} %get-tuple-element.1041) | copy-start | bytes 12292
  37.5 72.5 %copy-start.43 = (f32[1024]{0:T(1024)}, f32[1024]{0:T(1024)S(1)}, u32[]{:S(2)}) copy-start(f32[1024]{0:T(1024)S(1)} %get-tuple-element.1042) | copy-start | bytes 12292
  37.6 72.4 %copy-start.29 = (f32[2304]{0:T(1024)}, f32[2304]{0:T(1024)S(1)}, u32[]{:S(2)}) copy-start(f32[2304]{0:T(1024)S(1)} %get-tuple-element.910) | copy-start | bytes 27652
  37.6 72.4 %copy-start.31 = (f32[2304]{0:T(1024)}, f32[2304]{0:T(1024)S(1)}, u32[]{:S(2)}) copy-start(f32[2304]{0:T(1024)S(1)} %get-tuple-element.911) | copy-start | bytes 27652
  37.6 72.4 %copy-start.33 = (f32[2304]{0:T(1024)}, f32[2304]{0:T(1024)S(1)}, u32[]{:S(2)}) copy-start(f32[2304]{0:T(1024)S(1)} %get-tuple-element.912) | copy-start | bytes 27652
  37.6 72.4 %copy-start.35 = (f32[2304]{0:T(1024)}, f32[2304]{0:T(1024)S(1)}, u32[]{:S(2)}) copy-start(f32[2304]{0:T(1024)S(1)} %get-tuple-element.913) | copy-start | bytes 27652
  37.7 60.2 %copy-start.62 = (f32[32]{0:T(128)}, f32[32]{0:T(128)S(1)}, u32[]{:S(2)}) copy-start(f32[32]{0:T(128)S(1)} %fusion.151) | copy-start | bytes 388
  39.8 35.8 %copy-start.47 = (f32[1024]{0:T(1024)}, f32[1024]{0:T(1024)S(1)}, u32[]{:S(2)}) copy-start(f32[1024]{0:T(1024)S(1)} %fusion.119) | copy-start | bytes 12292
  39.8 35.7 %copy-start.55 = (f32[1024]{0:T(1024)}, f32[1024]{0:T(1024)S(1)}, u32[]{:S(2)}) copy-start(f32[1024]{0:T(1024)S(1)} %fusion.149) | copy-start | bytes 12292
  95.5 14.1 collective-permute-start
  110.0 24.1 %copy-start.9 = (f32[3,2304]{0,1:T(8,128)}, f32[3,2304]{0,1:T(8,128)S(1)}, u32[]{:S(2)}) copy-start(f32[3,2304]{0,1:T(8,128)S(1)} %copy.341) | copy-start | bytes 82948
  166.5 321.7 %copy-start.64 = (bf16[512]{0:T(512)(128)(2,1)S(1)}, bf16[512]{0:T(512)(128)(2,1)}, u32[]{:S(2)}) copy-start(bf16[512]{0:T(512)(128)(2,1)} %param.32) | copy-start | bytes 3076
  486.8 70.8 %all-gather.13.cloned.1.call-start = ((), (), s32[]{:S(2)}) async-start(), calls=%async_computation.1 | async-start | bytes 5242880 | tf_op jit(solution)/shard_map/all_gather | solution.py:183
  487.5 162.7 %all-gather.17.cloned.1.call-start = ((), (), s32[]{:S(2)}) async-start(), calls=%async_computation.4 | async-start | bytes 5242880 | tf_op jit(solution)/shard_map/all_gather | solution.py:30
  487.6 32.5 %copy-start.45 = (f32[1024]{0:T(1024)}, f32[1024]{0:T(1024)S(1)}, u32[]{:S(2)}) copy-start(f32[1024]{0:T(1024)S(1)} %fusion.148) | copy-start | bytes 12292
  493.8 123.3 %copy-start.50 = (f32[4,1,512]{2,1,0:T(1,128)}, f32[4,1,512]{2,1,0:T(1,128)S(1)}, u32[]{:S(2)}) copy-start(f32[4,1,512]{2,1,0:T(1,128)S(1)} %convert_element_type.176) | copy-start | bytes 24580
  509.3 84.0 %copy-start.16 = (f32[1024,32]{0,1:T(8,128)}, f32[1024,32]{0,1:T(8,128)S(1)}, u32[]{:S(2)}) copy-start(f32[1024,32]{0,1:T(8,128)S(1)} %exponential_multiply_fusion.4) | copy-start | bytes 393220
  521.7 133.1 %copy-start.2 = (f32[32,64,128]{2,1,0:T(8,128)}, f32[32,64,128]{2,1,0:T(8,128)S(1)}, u32[]{:S(2)}) copy-start(f32[32,64,128]{2,1,0:T(8,128)S(1)} %get-tuple-element.555) | copy-start | bytes 3145732
  551.1 66.0 %copy-start.57 = (f32[1024]{0:T(1024)}, f32[1024]{0:T(1024)S(1)}, u32[]{:S(2)}) copy-start(f32[1024]{0:T(1024)S(1)} %fusion.150) | copy-start | bytes 12292
  603.2 1451.1 %all-reduce.27.cloned.1.call-start = ((), (), s32[]{:S(2)}) async-start(), calls=%async_computation.5 | async-start | bytes 52809728
  697.5 27.2 %copy-start.8 = (f32[256,128]{1,0:T(8,128)}, f32[256,128]{1,0:T(8,128)S(1)}, u32[]{:S(2)}) copy-start(f32[256,128]{1,0:T(8,128)S(1)} %get-tuple-element.1306) | copy-start | bytes 393220 | tf_op jit(solution)/shard_map/transpose(jvp())/while
  708.5 16.2 copy-start.15
  757.4 60.3 %copy-start.7 = (f32[256,32]{1,0:T(8,128)S(1)}, f32[256,32]{1,0:T(8,128)}, u32[]{:S(2)}) copy-start(f32[256,32]{1,0:T(8,128)} %copy.513) | copy-start | bytes 98308 | tf_op jit(solution)/shard_map/transpose(jvp())/while
  847.2 27.2 %copy-start.8 = (f32[256,128]{1,0:T(8,128)}, f32[256,128]{1,0:T(8,128)S(1)}, u32[]{:S(2)}) copy-start(f32[256,128]{1,0:T(8,128)S(1)} %get-tuple-element.1306) | copy-start | bytes 393220 | tf_op jit(solution)/shard_map/transpose(jvp())/while
  858.2 16.1 copy-start.15
  907.1 60.3 %copy-start.7 = (f32[256,32]{1,0:T(8,128)S(1)}, f32[256,32]{1,0:T(8,128)}, u32[]{:S(2)}) copy-start(f32[256,32]{1,0:T(8,128)} %copy.513) | copy-start | bytes 98308 | tf_op jit(solution)/shard_map/transpose(jvp())/while
  996.9 27.2 %copy-start.8 = (f32[256,128]{1,0:T(8,128)}, f32[256,128]{1,0:T(8,128)S(1)}, u32[]{:S(2)}) copy-start(f32[256,128]{1,0:T(8,128)S(1)} %get-tuple-element.1306) | copy-start | bytes 393220 | tf_op jit(solution)/shard_map/transpose(jvp())/while
  1007.9 16.1 copy-start.15
  1056.8 60.3 %copy-start.7 = (f32[256,32]{1,0:T(8,128)S(1)}, f32[256,32]{1,0:T(8,128)}, u32[]{:S(2)}) copy-start(f32[256,32]{1,0:T(8,128)} %copy.513) | copy-start | bytes 98308 | tf_op jit(solution)/shard_map/transpose(jvp())/while
  1146.6 27.1 %copy-start.8 = (f32[256,128]{1,0:T(8,128)}, f32[256,128]{1,0:T(8,128)S(1)}, u32[]{:S(2)}) copy-start(f32[256,128]{1,0:T(8,128)S(1)} %get-tuple-element.1306) | copy-start | bytes 393220 | tf_op jit(solution)/shard_map/transpose(jvp())/while
  1157.6 16.1 copy-start.15
  1206.5 60.3 %copy-start.7 = (f32[256,32]{1,0:T(8,128)S(1)}, f32[256,32]{1,0:T(8,128)}, u32[]{:S(2)}) copy-start(f32[256,32]{1,0:T(8,128)} %copy.513) | copy-start | bytes 98308 | tf_op jit(solution)/shard_map/transpose(jvp())/while
  1299.4 18.3 slice-start
  1299.4 18.3 slice-start.1
  1307.5 11.6 slice-start.4
  1307.5 11.9 copy-start.10
  1307.5 11.9 copy-start.38
  1307.6 11.9 copy-start.40
  1307.6 11.9 copy-start.42
  1307.6 11.9 copy-start.44
  1319.5 24.0 %copy-start.30 = (f32[2304]{0:T(1024)S(1)}, f32[2304]{0:T(1024)}, u32[]{:S(2)}) copy-start(f32[2304]{0:T(1024)} %copy-done.29) | copy-start | bytes 27652
  1319.5 24.0 %copy-start.32 = (f32[2304]{0:T(1024)S(1)}, f32[2304]{0:T(1024)}, u32[]{:S(2)}) copy-start(f32[2304]{0:T(1024)} %copy-done.31) | copy-start | bytes 27652
  1319.5 24.0 %copy-start.34 = (f32[2304]{0:T(1024)S(1)}, f32[2304]{0:T(1024)}, u32[]{:S(2)}) copy-start(f32[2304]{0:T(1024)} %copy-done.33) | copy-start | bytes 27652
  1319.5 24.0 %copy-start.36 = (f32[2304]{0:T(1024)S(1)}, f32[2304]{0:T(1024)}, u32[]{:S(2)}) copy-start(f32[2304]{0:T(1024)} %copy-done.35) | copy-start | bytes 27652
  1414.4 12.0 copy-start.25
  1414.4 12.0 copy-start.61
  1414.5 12.0 copy-start.63
  1425.0 27.5 %collective-permute-start.1 = (f32[3,2304]{1,0:T(4,128)S(1)}, f32[3,2304]{1,0:T(4,128)S(1)}, u32[]{:S(2)}, u32[]{:S(2)}) collective-permute-start(f32[3,2304]{1,0:T(4,128)S(1)} %copy.370), channel_id=1, source_target_pairs={{1,0},{2,1},{3,2},{5,4},{6,5},{7,6},{9,8},{10,9},{11,10},{13,12},{... | collective-permute-start | bytes 82952 | tf_op jit(solution)/shard_map/ppermute | solution.py:23
  1426.4 12.4 slice-start.5
  1448.9 11.8 copy-start.11
  1448.9 11.8 copy-start.54
  1448.9 11.8 copy-start.56
  1545.0 17.8 copy-start.59
  1545.0 19.3 copy-start.52
  1609.7 733.7 %all-reduce.25.cloned.1.call-start = ((), (), s32[]{:S(2)}) async-start(), calls=%async_computation.2 | async-start | bytes 13205504 | tf_op jit(solution)/shard_map/psum | solution.py:271
  2054.4 66.9 %copy-start.51 = (f32[4,1,512]{2,1,0:T(1,128)S(1)}, f32[4,1,512]{2,1,0:T(1,128)}, u32[]{:S(2)}) copy-start(f32[4,1,512]{2,1,0:T(1,128)} %copy-done.50) | copy-start | bytes 24580
  2054.4 66.9 %copy-start.58 = (f32[1024]{0:T(1024)S(1)}, f32[1024]{0:T(1024)}, u32[]{:S(2)}) copy-start(f32[1024]{0:T(1024)} %copy-done.57) | copy-start | bytes 12292
  (35 other events, 240.3 us)
Sparse Core Ops, SparseCore 0:
  9.6 65.8 all-gather.10
  486.9 34.5 all-gather.14
  523.1 34.4 all-gather.12
  603.4 34.4 all-gather.16
  1609.8 444.5 all-reduce.26
  2121.4 221.9 all-reduce.24
where the time goes:
time: 2400 us; the launch traced here: 2380 us
  local copies, waits for them, and re-layouts  888 us (37%)
  waiting for transfers between devices  698 us (29%)
  matrix products  405 us (17%)
  other arithmetic  295 us (12%)
  loops' own time  38.6 us (2%)
  blocking collectives  30.4 us (1%)
    unnamed x7, waiting for transfers between devices  446 us
    dynamic_update_slice x24, local copies, waits for them, and re-layouts, scan_spans(): lax.scan(jax.checkpoint(span_step), zero_state, (split_up(xs_all), split_...  401 us
    psum x1, waiting for transfers between devices, body(): summed = lax.psum(mine[0], 'rep')  208 us
    dot_general x12, matrix products, span_step(): intra = jnp.einsum('hts,shp->thp', mixing, xs_part, precision=highest)  151 us
    unnamed x172, local copies, waits for them, and re-layouts  86.5 us
    another operation x39, other arithmetic  73.5 us
    squeeze x1, local copies, waits for them, and re-layouts, body(): summed = lax.psum(mine[0], 'rep')  66.8 us
    dot_general x12, matrix products, span_step(): jnp.einsum('sh,shp,sn->hpn', tail, xs_part, bmat, precision=highest)  59.5 us
  transfers between devices with their start and end apart: 8, of which 5 were waited for; matrix products, arithmetic and copies ran while one was open for 7% of the time, Pallas kernels for 0%

commit v1 on v0

v1 whole, which is shorter than its diff:
```python
import jax
import jax.numpy as jnp
from jax import lax
from jax.sharding import PartitionSpec as P

H = 32
P_SIZE = 64
N = 128
E = 2048
CHUNK = 128
RESET = 128.0

highest = lax.Precision.HIGHEST
epsilon = 1e-05
low = jnp.bfloat16
wide = jnp.float32


def shifted(x, axis, by):
    peers = lax.axis_size(axis)
    pairs = [(i, i + by) for i in range(peers) if 0 <= i + by < peers]
    return lax.ppermute(x, axis, pairs)


def swapped(x, axis, bit):
    return lax.ppermute(x, axis, [(i, i ^ bit) for i in range(lax.axis_size(axis))])


def mm(spec, a, b):
    return jnp.einsum(spec, a.astype(low), b.astype(low), preferred_element_type=wide)


def exact(spec, a, b):
    return jnp.einsum(spec, a, b, precision=highest, preferred_element_type=wide)


def gather_rows(x, axis):
    count, me = lax.axis_size(axis), lax.axis_index(axis)
    held = x[None]
    bit = count // 2
    while bit >= 1:
        other = swapped(held, axis, bit)
        mine_first = (me & bit) == 0
        pair = jnp.stack(
            [jnp.where(mine_first, held, other), jnp.where(mine_first, other, held)], axis=1
        )
        held = pair.reshape((-1,) + x.shape)
        bit //= 2
    return held.reshape((count * x.shape[0],) + x.shape[1:])


def reduce_rows(partial):
    owners, mine = lax.axis_size("fsdp"), lax.axis_index("fsdp")
    held = partial.reshape((owners, partial.shape[0] // owners) + partial.shape[1:])
    bit = 1
    while bit < owners:
        pair = held.reshape((held.shape[0] // 2, 2) + held.shape[1:])
        side = (mine // bit) % 2
        keep = lax.dynamic_index_in_dim(pair, side, 1, False)
        send = lax.dynamic_index_in_dim(pair, 1 - side, 1, False).astype(low)
        held = keep + swapped(send, "fsdp", bit).astype(wide)
        bit *= 2
    held = held[0]
    copies, here = lax.axis_size("rep"), lax.axis_index("rep")
    bit = 1
    while bit < copies:
        half = held.shape[0] // 2
        side = (here // bit) % 2
        keep = lax.dynamic_slice_in_dim(held, side * half, half, 0)
        send = lax.dynamic_slice_in_dim(held, (1 - side) * half, half, 0).astype(low)
        held = keep + swapped(send, "rep", bit).astype(wide)
        bit *= 2
    held = held.astype(low)
    while bit > 1:
        bit //= 2
        other = swapped(held, "rep", bit)
        lower = ((here // bit) % 2) == 0
        held = jnp.concatenate(
            [jnp.where(lower, held, other), jnp.where(lower, other, held)], axis=0
        )
    return held.astype(wide)


def silu_parts(x):
    s = jax.nn.sigmoid(x)
    return x * s, s * (1.0 + x * (1.0 - s))


def body(
    tokens,
    norm_w,
    in_w,
    conv_w,
    conv_b,
    dt_bias,
    a_log,
    d_skip,
    gnorm_w,
    out_w,
    first_length,
    cotangent,
):
    ranks, rank = lax.axis_size("fsdp"), lax.axis_index("fsdp")
    length = tokens.shape[0]
    count = length // CHUNK
    taps = conv_w.shape[0]
    smalls = (norm_w, conv_w.T, conv_b, dt_bias, a_log, d_skip, gnorm_w)
    flat = lax.all_gather(jnp.concatenate([v.reshape(-1) for v in smalls]), "fsdp", axis=0)
    flat = flat.astype(wide)
    parts, at = [], 0
    for v in smalls:
        parts.append(flat[:, at : at + v.size].reshape((ranks * v.shape[0],) + v.shape[1:]))
        at += v.size
    norm32, conv32, bias32, dt32, alog32, skip32, gnorm32 = parts
    conv32 = conv32.T
    w_x = gather_rows(in_w[:, E:], "fsdp")
    in_z, out_s, w_x = lax.optimization_barrier((in_w[:, :E], out_w, w_x))
    w_z = gather_rows(in_z, "fsdp")
    w_out = gather_rows(out_s, "fsdp")

    first_place = rank * length
    places = first_place + jnp.arange(length + taps - 1, dtype=jnp.int32)
    boundary = first_length[0]
    starts = jnp.where(places >= boundary, boundary, jnp.zeros_like(boundary))

    def tap_valid(index, lo, hi):
        ok = places[lo:hi] - (taps - 1) + index >= starts[lo:hi]
        return ok.astype(wide)[:, None]

    u = tokens.astype(wide)
    scale_in = lax.rsqrt(jnp.mean(u * u, axis=-1, keepdims=True) + epsilon)
    normed = (u * scale_in * norm32[None, :]).astype(low)
    proj_x = jnp.dot(normed, w_x, preferred_element_type=wide)
    xbc = proj_x[:, : E + 2 * N]
    rim = shifted(xbc[length - (taps - 1) :], "fsdp", 1)

    full = jnp.concatenate([rim, xbc], axis=0)
    pre = jnp.zeros_like(xbc) + bias32[None, :]
    for k in range(taps):
        pre = pre + full[k : k + length] * conv32[k][None, :] * tap_valid(k, 0, length)
    xc = pre * jax.nn.sigmoid(pre)

    draw = proj_x[:, E + 2 * N :] + dt32[None, :]
    delta_rows = jax.nn.softplus(draw)
    reset = RESET * (places[:length] == boundary).astype(wide)
    rate = -jnp.exp(alog32)

    def by_head(v):
        return v.reshape(count, CHUNK, H).transpose(0, 2, 1)

    delta = by_head(delta_rows)
    decay = delta * rate[None, :, None] - reset.reshape(count, 1, CHUNK)
    spots = jnp.arange(CHUNK)
    upto = (spots[:, None] <= spots[None, :]).astype(wide)
    cum = exact("chs,st->cht", decay, upto)
    last = cum[:, :, -1]
    growth = jnp.exp(last)
    totals = lax.all_gather(jnp.exp(jnp.sum(last, axis=0)), "fsdp", axis=0)
    entry = jnp.exp(cum)[:, :, None, :]
    tail = jnp.exp(last[:, :, None] - cum)[:, :, None, :]

    def heads(v):
        return v.reshape(count, H, P_SIZE, CHUNK)

    def flatten(v):
        return v.reshape(count, E, CHUNK)

    def turned(v):
        return heads(v.reshape(count, CHUNK, E).transpose(0, 2, 1))

    def turned_back(v):
        return flatten(v).transpose(0, 2, 1).reshape(length, E)

    x = turned(xc[:, :E])
    bmat = xc[:, E : E + N].reshape(count, CHUNK, N)
    cmat = xc[:, E + N :].reshape(count, CHUNK, N)
    xd = x * delta[:, :, None, :]
    xd_low = xd.astype(low)
    xw = (xd * tail).astype(low)
    state_own = mm("ceq,cqn->cen", flatten(xw), bmat).reshape(count, H, P_SIZE, N)

    def widen(v):
        return v[:, None, None]

    entering = [jnp.zeros((H, P_SIZE, N), wide)]
    before = [jnp.ones((H,), wide)]
    for c in range(count):
        entering.append(entering[c] * widen(growth[c]) + state_own[c])
        before.append(before[c] * growth[c])
    final = entering[count].astype(low)

    def incoming(value, sign):
        total, factor = jnp.zeros(value.shape, wide), jnp.ones((H,), wide)
        for j in range(1, ranks):
            got = shifted(value, "fsdp", sign * j).astype(wide)
            total = total + got * widen(factor)
            source = jnp.clip(rank - sign * j, 0, ranks - 1)
            factor = factor * lax.dynamic_index_in_dim(totals, source, 0, False)
        return total

    inflow = incoming(final, 1)
    state = jnp.stack([entering[c] + inflow * widen(before[c]) for c in range(count)])

    inner = exact("ctn,csn->cts", cmat, bmat)
    causal = (spots[:, None] >= spots[None, :])[None, None]
    spread = jnp.where(causal, cum[:, :, :, None] - cum[:, :, None, :], -1e30)
    fade = jnp.exp(spread)
    mixing = (fade * inner[:, None]).astype(low)
    state_low = state.astype(low).reshape(count, E, N)
    from_state = heads(mm("cen,ctn->cet", state_low, cmat)) * entry
    y_t = (
        mm("chps,chts->chpt", xd_low, mixing)
        + from_state
        + x * skip32[None, :, None, None]
    )
    y = turned_back(y_t)

    z = jnp.dot(normed, w_z, preferred_element_type=wide)
    silu_z, slope_z = silu_parts(z)
    g = y * silu_z
    scale_g = lax.rsqrt(jnp.mean(g * g, axis=-1, keepdims=True) + epsilon)
    hat = g * scale_g
    gated = (hat * gnorm32[None, :]).astype(low)
    output = (u + jnp.dot(gated, w_out, preferred_element_type=wide)).astype(low)

    d_gated = jnp.dot(cotangent, w_out.T, preferred_element_type=wide)
    d_out_w = reduce_rows(mm("te,td->ed", gated, cotangent))
    d_gnorm = jnp.sum(d_gated * hat, axis=0)
    d_hat = d_gated * gnorm32[None, :]
    d_g = scale_g * (d_hat - hat * jnp.mean(d_hat * hat, axis=-1, keepdims=True))
    d_y = d_g * silu_z
    d_z = (d_g * y * slope_z).astype(low)
    d_in_z = reduce_rows(mm("td,te->de", normed, d_z))

    dy = turned(d_y)
    dy_low = dy.astype(low)
    d_skip_own = jnp.sum(x * dy, axis=(0, 2, 3))
    faded = (dy * entry).astype(low)
    direct = mm("cet,ctn->cen", flatten(faded), cmat).reshape(count, H, P_SIZE, N)
    leaving = [None] * count + [jnp.zeros((H, P_SIZE, N), wide)]
    after = [None] * count + [jnp.ones((H,), wide)]
    for c in reversed(range(count)):
        leaving[c] = leaving[c + 1] * widen(growth[c]) + direct[c]
        after[c] = after[c + 1] * growth[c]
    outflow = incoming(leaving[0].astype(low), -1)
    d_state = jnp.stack([leaving[c + 1] + outflow * widen(after[c + 1]) for c in range(count)])
    d_state_low = d_state.astype(low).reshape(count, E, N)

    d_mix = mm("chpt,chps->chts", dy_low, xd_low) * fade
    d_inner = jnp.sum(d_mix, axis=1)
    weight = d_mix * inner[:, None]
    d_cum = jnp.sum(weight, axis=3) - jnp.sum(weight, axis=2) + jnp.sum(dy * from_state, axis=2)
    pulled = heads(mm("cen,cqn->ceq", d_state_low, bmat)) * tail
    d_xd = mm("chts,chpt->chps", mixing, dy_low) + pulled
    d_tail = jnp.sum(xd * pulled, axis=2)
    d_keep = growth * jnp.sum(state * d_state, axis=(2, 3))
    d_decay = (
        exact("cht,st->chs", d_cum, upto)
        + exact("chs,st->cht", d_tail, upto - jnp.eye(CHUNK, dtype=wide))
        + d_keep[:, :, None]
    )
    d_delta = jnp.sum(x * d_xd, axis=2) + d_decay * rate[None, :, None]
    d_alog = jnp.sum(d_decay * delta, axis=(0, 2)) * rate
    d_x = turned_back(d_xd * delta[:, :, None, :] + dy * skip32[None, :, None, None])
    d_c = mm("cts,csn->ctn", d_inner, bmat) + mm("cet,cen->ctn", flatten(faded), state_low)
    d_b = mm("cts,ctn->csn", d_inner, cmat) + mm("ceq,cen->cqn", flatten(xw), d_state_low)
    d_draw = d_delta.transpose(0, 2, 1).reshape(length, H) * jax.nn.sigmoid(draw)
    d_dt = jnp.sum(d_draw, axis=0)

    d_xc = jnp.concatenate([d_x, d_b.reshape(length, N), d_c.reshape(length, N)], axis=1)
    d_pre = d_xc * silu_parts(pre)[1]
    d_rim = shifted(d_pre[: taps - 1], "fsdp", -1)
    d_bias = jnp.sum(d_pre, axis=0)
    d_conv = jnp.stack(
        [
            jnp.sum(d_pre * tap_valid(k, 0, length) * full[k : k + length], axis=0)
            for k in range(taps)
        ]
    )
    d_full = jnp.concatenate([d_pre, d_rim], axis=0)
    d_xbc = jnp.zeros_like(xbc)
    for k in range(taps):
        lo = taps - 1 - k
        d_xbc = d_xbc + d_full[lo : lo + length] * conv32[k][None, :] * tap_valid(
            k, lo, lo + length
        )
    d_proj_x = jnp.concatenate([d_xbc.astype(low), d_draw.astype(low)], axis=1)
    d_in_x = reduce_rows(mm("td,te->de", normed, d_proj_x))
    d_normed = mm("te,de->td", d_z, w_z) + mm("te,de->td", d_proj_x, w_x)
    hat_in = u * scale_in
    d_norm = jnp.sum(d_normed * hat_in, axis=0)
    d_hat_in = d_normed * norm32[None, :]
    d_tokens = cotangent.astype(wide) + scale_in * (
        d_hat_in - hat_in * jnp.mean(d_hat_in * hat_in, axis=-1, keepdims=True)
    )

    owned = (d_norm, d_conv.T, d_bias, d_dt, d_alog, d_skip_own, d_gnorm)
    stacked = jnp.concatenate([v.reshape(ranks, -1) for v in owned], axis=1)
    summed = lax.psum(stacked, ("rep", "fsdp"))
    mine = lax.dynamic_index_in_dim(summed, rank, 0, False)
    grads, at = [], 0
    for v in smalls:
        grads.append(mine[at : at + v.size].reshape(v.shape))
        at += v.size
    g_norm, g_conv, g_bias, g_dt, g_alog, g_skip, g_gnorm = grads
    return (
        output,
        d_tokens,
        g_norm,
        jnp.concatenate([d_in_z, d_in_x], axis=1),
        g_conv.T,
        g_bias,
        g_dt,
        g_alog,
        g_skip,
        g_gnorm,
        d_out_w,
    )


def solution(mesh):
    in_specs = (
        P(("rep", "fsdp"), None),
        P("fsdp"),
        P("fsdp", None),
        P(None, "fsdp"),
        P("fsdp"),
        P("fsdp"),
        P("fsdp"),
        P("fsdp"),
        P("fsdp"),
        P("fsdp", None),
        P("rep"),
        P(("rep", "fsdp"), None),
    )
    out_specs = (
        P(("rep", "fsdp"), None),
        P(("rep", "fsdp"), None),
        P("fsdp"),
        P("fsdp", None),
        P(None, "fsdp"),
        P("fsdp"),
        P("fsdp"),
        P("fsdp"),
        P("fsdp"),
        P("fsdp"),
        P("fsdp", None),
    )
    return jax.shard_map(body, mesh=mesh, in_specs=in_specs, out_specs=out_specs, check_vma=False)
```

time: 2400 us -> 817 us (0.34)
  local copies, waits for them, and re-layouts: 888 us -> 203 us
  waiting for transfers between devices: 698 us -> 145 us
  matrix products: 405 us -> 139 us
  other arithmetic: 295 us -> 193 us
  blocking collectives: 30.4 us -> 78.4 us
  loops' own time: 38.6 us -> 0 us
  starting transfers between devices: 3.87 us -> 41.3 us
    unnamed x7 -> x0, waiting for transfers between devices: 446 us -> none
    dynamic_update_slice x24 -> x0, local copies, waits for them, and re-layouts: 401 us -> none  [scan_spans(): lax.scan(jax.checkpoint(span_step), zero_state, (split_up(xs_all), split_...]
    dot_general x65 -> x24, matrix products: 405 us -> 139 us  [the longest x16 101 us: mm(): jnp.einsum(spec, a.astype(low), b.astype(low), preferred_element_type=wide)]
    psum x1 -> x0, waiting for transfers between devices: 208 us -> none  [body(): summed = lax.psum(mine[0], 'rep')]
    ppermute x0 -> x30, waiting for transfers between devices: none -> 145 us  [swapped(): lax.ppermute(x, axis, [(i, i ^ bit) for i in range(lax.axis_size(axis))])]
    squeeze x17 -> x0, local copies, waits for them, and re-layouts: 99.5 us -> none  [the longest x1 66.8 us: body(): summed = lax.psum(mine[0], 'rep')]
    convert_element_type x17 -> x11, other arithmetic: 10.9 us -> 64.3 us  [the longest x1 23.8 us: body(): d_proj_x = jnp.concatenate([d_xbc.astype(low), d_draw.astype(low)], axis=1)]
    another operation x39 -> x12, other arithmetic: 73.5 us -> 22 us  [the longest x9 20.3 us: gather_rows(): jnp.stack([jnp.where(mine_first, held, other), jnp.where(mine_first, othe...]
  transfers between devices with their start and end apart: 8 -> 38, of which waited for: 5 -> 14; matrix products, arithmetic and copies ran while one was open for 7% -> 50% of each run, Pallas kernels for 0% -> 0%
where the time goes in v1:
time: 817 us; the launch traced here: 805 us
  local copies, waits for them, and re-layouts  203 us (25%)
  other arithmetic  193 us (24%)
  waiting for transfers between devices  145 us (18%)
  matrix products  139 us (17%)
  blocking collectives  78.4 us (10%)
  starting transfers between devices  41.3 us (5%)
    ppermute x30, waiting for transfers between devices, swapped(): lax.ppermute(x, axis, [(i, i ^ bit) for i in range(lax.axis_size(axis))])  145 us
    dot_general x16, matrix products, mm(): jnp.einsum(spec, a.astype(low), b.astype(low), preferred_element_type=wide)  101 us
    psum x1, blocking collectives, body(): summed = lax.psum(stacked, ('rep', 'fsdp'))  44.7 us
    unnamed x337, local copies, waits for them, and re-layouts  35.6 us
    unnamed x2, blocking collectives  33.7 us
    ppermute x30, starting transfers between devices, swapped(): lax.ppermute(x, axis, [(i, i ^ bit) for i in range(lax.axis_size(axis))])  26.9 us
    mul x1, other arithmetic, body(): xc = pre * jax.nn.sigmoid(pre)  24.1 us
    convert_element_type x1, other arithmetic, body(): d_proj_x = jnp.concatenate([d_xbc.astype(low), d_draw.astype(low)], axis=1)  23.8 us
  transfers between devices with their start and end apart: 38, of which 14 were waited for; matrix products, arithmetic and copies ran while one was open for 50% of the time, Pallas kernels for 0%

profile of v1, /device:TPU:0, one launch (start us, length us, event | category | flops | bytes accessed | tf_op | source)
XLA Modules:
  0.0 804.9 jit_solution(12253641708394447491)
XLA Ops:
  5.1 26.4 %collective-permute-done = bf16[1,256,2336]{1,2,0:T(8,128)(2,1)} collective-permute-done((bf16[1,256,2336]{1,2,0:T(8,128)(2,1)S(1)}, bf16[1,256,2336]{1,2,0:T(8,128)(2,1)}, u32[]{:S(2)}, u32[]{:S(2)}) %collective-permute-start) | collective-permute-done | bytes 1196064 | tf_op jit(solution)/shard_map/ppermute | solution.py:26
  38.0 12.0 %all-reduce = bf16[14688]{0:T(1024)(128)(2,1)S(1)} all-reduce(bf16[14688]{0:T(1024)(128)(2,1)S(1)} %dynamic-update-slice), channel_id=2, replica_groups=mesh['rep'=8,'fsdp'=4] {'fsdp'}, use_global_device_ids=true, to_apply=%add | all-reduce | flops 14688 | bytes 58752
  64.6 7.5 copy.249
  72.1 7.7 fusion.128
  86.9 9.3 %slice.355 = f32[1024,2304]{0,1:T(8,128)} slice(f32[1024,2336]{0,1:T(8,128)} %copy-done.2), slice={[0:1024], [0:2304]} | slice | bytes 18874368 | tf_op jit(solution)/shard_map/slice | solution.py:134
  98.2 3.8 mul.977
  101.9 9.2 %copy.258 = f32[8,2048,128]{1,2,0:T(8,128)} copy(f32[8,2048,128]{2,1,0:T(8,128)} %bitcast.426) | data formatting | bytes 16777216 | tf_op jit(solution)/shard_map/mul | solution.py:179
  111.1 3.8 mul.964
  114.9 9.2 %copy.257 = f32[8,2048,128]{1,2,0:T(8,128)} copy(f32[8,2048,128]{2,1,0:T(8,128)} %bitcast.427) | data formatting | bytes 16777216 | tf_op jit(solution)/shard_map/mul | solution.py:177
  124.5 24.1 %fusion.15 = (f32[1024,2304]{0,1:T(8,128)S(1)}, f32[1024,2304]{0,1:T(8,128)}) fusion(f32[1024]{0:T(1024)S(1)} %get-tuple-element.226, f32[1024,2304]{0,1:T(8,128)} %slice.355, f32[2304]{0:T(1024)S(1)} %get-tuple-element.101, f32[1024]{0:T(1024)S(1)} %get-tuple-element.225, f32[2304]{0:T(1024)S(1)} %get-tuple-element.102, f32[3,2304]{0,1:T(8,128)S(1)} %copy.251, ...), kind=kLoop, calls=%fused_computation.35 | loop fusion | flops 44826624 | bytes 28401664 | tf_op jit(solution)/shard_map/mul | solution.py:141
  149.6 4.1 slice.367
  153.6 9.2 %copy.291 = f32[1024,2048]{1,0:T(8,128)} copy(f32[1024,2048]{0,1:T(8,128)} %slice.367) | data formatting | bytes 16777216 | tf_op jit(solution)/shard_map/reshape | solution.py:169
  163.0 9.5 %multiply_convert_fusion.5 = bf16[8,2048,128]{1,2,0:T(8,128)(2,1)S(1)} fusion(f32[8,2048,128]{1,2,0:T(8,128)} %copy.258, f32[8,2048,128]{1,2,0:T(8,128)} %bitcast.410, f32[8,2048,128]{1,2,0:T(8,128)} %copy.257), kind=kLoop, calls=%fused_computation.61 | loop fusion | flops 6291456 | bytes 29360128 | tf_op jit(solution)/shard_map/convert_element_type | solution.py:179
  176.3 3.8 add_convert_fusion.1
  187.6 21.7 %all-reduce.1 = f32[128]{0:T(128)S(1)} all-reduce(f32[128]{0:T(128)S(1)} %exponential_dynamic-update-slice_fusion), channel_id=3, replica_groups=mesh['rep'=8,'fsdp'=4] {'fsdp'}, use_global_device_ids=true, to_apply=%add.1 | all-reduce | flops 128 | bytes 1024
  209.3 3.8 mul.1027
  213.1 9.1 %copy.266 = f32[8,2048,128]{1,2,0:T(8,128)} copy(f32[8,2048,128]{2,1,0:T(8,128)} %bitcast.428) | data formatting | bytes 16777216 | tf_op jit(solution)/shard_map/mul | solution.py:210
  222.8 9.2 %copy.253 = f32[8,2048,128]{2,1,0:T(8,128)} copy(f32[8,2048,128]{1,2,0:T(8,128)} %bitcast.411) | data formatting | bytes 16777216 | tf_op jit(solution)/shard_map/transpose | solution.py:169
  243.3 3.7 select_bitcast_fusion.11
  252.1 3.4 slice-done.14
  255.5 9.4 %multiply_add_fusion.2 = f32[8,32,64,128]{3,2,1,0:T(8,128)} fusion(f32[8,32,64,128]{3,2,1,0:T(8,128)S(1)} %bitcast.462, f32[8,32,64,128]{3,2,1,0:T(8,128)S(1)} %bitcast.424, f32[32]{0:T(128)S(1)} %copy-done.133, f32[8,32,128]{2,1,0:T(8,128)S(1)} %get-tuple-element.215, f32[8,128,128]{2,1,0:T(8,128)S(1)} %fusion.153, f32[8,32,128]{2,1,0:T(8,128)S(1)} %fusion.68, ...), kind=kOutput, calls=%fused_computation.60 | convolution fusion | flops 566231040 | bytes 26099840 | tf_op jit(solution)/shard_map/chps,chts->chpt/dot_general | solution.py:30
  264.9 9.1 %copy.262 = f32[8,128,2048]{2,1,0:T(8,128)} copy(f32[8,128,2048]{1,2,0:T(8,128)} %bitcast.465) | data formatting | bytes 16777216 | tf_op jit(solution)/shard_map/transpose | solution.py:172
  283.1 11.0 %multiply_reduce_fusion.12 = (f32[1024]{0:T(1024)S(1)}, f32[1024,2048]{1,0:T(8,128)S(1)}, f32[1024,2048]{1,0:T(8,128)}) fusion(f32[8,128,2048]{2,1,0:T(8,128)S(1)} %bitcast.430, bf16[1024,2048]{1,0:T(8,128)(2,1)} %bitcast.476, bf16[1024,1024]{1,0:T(8,128)(2,1)} %param.12, f32[1024]{0:T(1024)S(1)} %bitcast.513, f32[1024]{0:T(1024)S(1)} %add_rsqrt_fusion.1), kind=kOutput, calls=%fused_computation.57 | convolution fusion | flops 4313840640 | bytes 31469568 | tf_op jit(solution)/shard_map/dot_general | solution.py:218
  294.1 3.7 select_bitcast_fusion.3
  299.4 6.0 fusion.43
  305.5 8.2 %fusion.18 = (f32[2048]{0:T(1024)}, f32[1024]{0:T(1024)S(1)}, f32[2048,1024]{0,1:T(8,128)}) fusion(f32[1024,2048]{1,0:T(8,128)S(1)} %get-tuple-element.139, f32[1024]{0:T(1024)S(1)} %add_rsqrt_fusion, f32[2048]{0:T(1024)S(1)} %bitcast.508, bf16[2048,1024]{1,0:T(8,128)(2,1)S(1)} %bitcast.479, bf16[1024,1024]{1,0:T(8,128)(2,1)S(1)} %copy-done.40), kind=kOutput, calls=%fused_computation.42 | convolution fusion | flops 4307547136 | bytes 23093248 | tf_op jit(solution)/shard_map/dot_general | solution.py:226
  313.7 15.5 %fusion.20 = bf16[1024,2048]{1,0:T(8,128)(2,1)} fusion(f32[8,128,2048]{2,1,0:T(8,128)} %copy.262, f32[1024,2048]{1,0:T(8,128)} %get-tuple-element.248, f32[1024]{0:T(1024)S(1)} %broadcast_multiply_fusion, f32[1024,2048]{1,0:T(8,128)} %copy-done.5, f32[2048,1024]{0,1:T(8,128)} %get-tuple-element.249, f32[2048]{0:T(1024)S(1)} %bitcast.509, ...), kind=kLoop, calls=%fused_computation.46 | loop fusion | flops 31457280 | bytes 37765120 | tf_op jit(solution)/shard_map/convert_element_type | solution.py:232
  329.3 13.1 %multiply_reduce_fusion.6 = (f32[2048]{0:T(1024)S(1)}, f32[1024,2048]{1,0:T(8,128)}) fusion(f32[1024,2048]{1,0:T(8,128)S(1)} %bitcast.413, f32[1024,2048]{1,0:T(8,128)} %get-tuple-element.248, f32[1024]{0:T(1024)S(1)} %broadcast_multiply_fusion, f32[1024,2048]{1,0:T(8,128)} %copy-done.5, f32[2048]{0:T(1024)S(1)} %bitcast.510, ...), kind=kLoop, calls=%fused_computation.47 | loop fusion | flops 25163776 | bytes 41967616 | tf_op jit(solution)/shard_map/reduce_sum | solution.py:237
  342.4 10.5 %fusion.122 = f32[2048,1024]{1,0:T(8,128)} fusion(bf16[1024,1024]{1,0:T(8,128)(2,1)S(1)} %copy-done.41, f32[1024,2048]{1,0:T(8,128)} %copy-done.5, f32[2048]{0:T(1024)S(1)} %bitcast.511, f32[1024]{0:T(1024)S(1)} %add_rsqrt_fusion), kind=kOutput, calls=%fused_computation.369 | convolution fusion | flops 4301258752 | bytes 18886656 | tf_op jit(solution)/shard_map/te,td->ed/dot_general | solution.py:30
  352.9 9.1 %copy.265 = f32[8,2048,128]{2,1,0:T(8,128)} copy(f32[8,2048,128]{1,2,0:T(8,128)} %bitcast.416) | data formatting | bytes 16777216 | tf_op jit(solution)/shard_map/transpose | solution.py:169
  362.0 7.2 multiply_convert_fusion.3
  369.2 4.3 fusion.155
  382.8 9.3 %multiply_reduce_fusion.9 = f32[8,32,128]{2,1,0:T(8,128)} fusion(f32[8,2048,128]{2,1,0:T(8,128)} %copy-done.4, f32[8,32,128]{2,1,0:T(8,128)S(1)} %get-tuple-element.215, f32[8,2048,128]{2,1,0:T(8,128)} %copy.265), kind=kLoop, calls=%fused_computation.50 | loop fusion | flops 6258688 | bytes 17039360 | tf_op jit(solution)/shard_map/reduce_sum | solution.py:252
  393.0 16.7 %multiply_reduce_fusion = (f32[8,32,128]{2,1,0:T(8,128)}, f32[8,32,128]{2,1,0:T(8,128)}, bf16[8,128,128]{2,1,0:T(8,128)(2,1)S(1)}) fusion(f32[8,128,128]{2,1,0:T(8,128)} %copy-done.48, f32[8,32,128]{2,1,0:T(8,128)S(1)} %fusion.68, pred[128,128]{1,0:T(8,128)(4,1)} %iota_compare_fusion.3, f32[8,32,64,128]{3,2,1,0:T(8,128)} %bitcast.459, ...), kind=kOutput, calls=%fused_computation.3 | convolution fusion | flops 572325888 | bytes 18104320 | tf_op jit(solution)/shard_map/chpt,chps->chts/dot_general | solution.py:30
  412.8 3.9 fusion.49
  418.0 7.4 fusion.124
  436.9 4.5 fusion.101
  441.9 4.4 multiply_reduce_fusion.7
  447.3 18.1 %multiply_reduce_fusion.8 = (f32[8,32,128]{2,1,0:T(8,128)S(1)}, f32[8,32,128]{2,1,0:T(8,128)S(1)}, f32[8,32,64,128]{3,2,1,0:T(8,128)}) fusion(f32[8,2048,128]{2,1,0:T(8,128)} %fusion.101, f32[8,2048,128]{2,1,0:T(8,128)} %copy.253, f32[8,32,128]{2,1,0:T(8,128)S(1)} %copy-done.46, f32[8,32,128]{2,1,0:T(8,128)S(1)} %bitcast_bitcast_fusion, ...), kind=kOutput, calls=%fused_computation.49 | convolution fusion | flops 578748416 | bytes 43139200 | tf_op jit(solution)/shard_map/chts,chpt->chps/dot_general | solution.py:30
  468.0 11.0 %copy.268 = f32[8,2048,128]{2,0,1:T(8,128)} copy(f32[8,2048,128]{2,1,0:T(8,128)} %bitcast.464) | data formatting | bytes 16777216 | tf_op jit(solution)/shard_map/reshape | solution.py:166
  479.0 8.9 %copy.318 = f32[256,8,8,128]{3,1,2,0:T(8,128)} copy(f32[256,8,8,128]{3,2,1,0:T(8,128)} %bitcast.425) | data formatting | bytes 16777216
  488.0 19.0 %fusion.130 = (f32[2304]{0:T(1024)S(1)}, f32[2304]{0:T(1024)S(1)}, f32[2304]{0:T(1024)S(1)}, f32[2304]{0:T(1024)S(1)}, f32[2304]{0:T(1024)S(1)}, /*index=5*/f32[1024,2304]{0,1:T(8,128)}) fusion(f32[1024,2336]{0,1:T(8,128)S(1)} %bitcast.419, f32[1024]{0:T(1024)S(1)} %copy-done.64, f32[1024,2304]{0,1:T(8,128)S(1)} %bitcast.415, f32[3,2304]{0,1:T(8,128)S(1)} %copy-done.17, ...), kind=kLoop, calls=%fused_computation.373 | loop fusion | flops 61330176 | bytes 47276032 | tf_op jit(solution)/shard_map/reduce_sum | solution.py:273
  512.8 23.8 %fusion.7 = bf16[1024,2304]{0,1:T(8,128)(2,1)S(1)} fusion(f32[1024,2304]{0,1:T(8,128)} %get-tuple-element.110, f32[3,2304]{0,1:T(8,128)S(1)} %copy.273, f32[1024]{0:T(1024)S(1)} %copy-done.78, f32[1024]{0:T(1024)S(1)} %copy-done.79, f32[1024]{0:T(1024)S(1)} %copy-done.77, f32[1024]{0:T(1024)S(1)} %copy-done.64, f32[2304]{0:T(1024)S(1)} %copy-done.57, ...), kind=kLoop, calls=%fused_computation.19 | loop fusion | flops 35389440 | bytes 14236672 | tf_op jit(solution)/shard_map/convert_element_type | solution.py:287
  536.6 7.8 fusion.46
  544.4 8.4 %fusion.45 = f32[1024,2336]{0,1:T(8,128)} fusion(bf16[1024,32]{0,1:T(8,128)(2,1)S(1)} %get-tuple-element.109, bf16[1024,2304]{0,1:T(8,128)(2,1)S(1)} %fusion.7, bf16[1024,1024]{1,0:T(8,128)(2,1)S(1)} %copy-done.33, f32[1024]{0:T(1024)S(1)} %bitcast.515, f32[1024]{0:T(1024)S(1)} %copy-done.74), kind=kOutput, calls=%fused_computation.100 | convolution fusion | flops 4912709632 | bytes 16457728 | tf_op jit(solution)/shard_map/td,te->de/dot_general | solution.py:30
  552.9 6.8 fusion.41
  559.8 44.7 %psum.7 = f32[4,3672]{1,0:T(4,128)S(1)} all-reduce(f32[4,3672]{1,0:T(4,128)S(1)} %concatenate.60), channel_id=1, replica_groups=mesh['rep'=8,'fsdp'=4] {'rep','fsdp'}, use_global_device_ids=true, to_apply=%region_23.24 | all-reduce | flops 14688 | bytes 117504 | tf_op jit(solution)/shard_map/psum | solution.py:299
  606.3 13.4 %reshape_reshape.22 = f32[2,2,256,2336]{2,1,0,3:T(2,128)} reshape(f32[1024,2336]{0,1:T(8,128)} %fusion.45) | data formatting | bytes 19136512 | tf_op jit(solution)/shard_map/reshape;reshape | solution.py:57
  619.7 7.5 constant_dynamic-slice_fusion.2
  634.4 4.3 constant_dynamic-slice_fusion.3
  648.9 19.1 %collective-permute-done.31 = bf16[1,512,1024]{2,1,0:T(8,128)(2,1)S(1)} collective-permute-done((bf16[1,512,1024]{2,1,0:T(8,128)(2,1)S(1)}, bf16[1,512,1024]{2,1,0:T(8,128)(2,1)S(1)}, u32[]{:S(2)}, u32[]{:S(2)}) %collective-permute-start.31) | collective-permute-done | bytes 1048608 | tf_op jit(solution)/shard_map/ppermute | solution.py:26
  670.4 19.8 %collective-permute-done.15 = bf16[1,256,2048]{2,1,0:T(8,128)(2,1)S(1)} collective-permute-done((bf16[1,256,2048]{2,1,0:T(8,128)(2,1)S(1)}, bf16[1,256,2048]{2,1,0:T(8,128)(2,1)S(1)}, u32[]{:S(2)}, u32[]{:S(2)}) %collective-permute-start.15) | collective-permute-done | bytes 1048608 | tf_op jit(solution)/shard_map/ppermute | solution.py:26
  694.9 9.5 %collective-permute-done.16 = bf16[128,2048]{1,0:T(8,128)(2,1)S(1)} collective-permute-done((bf16[128,2048]{1,0:T(8,128)(2,1)S(1)}, bf16[128,2048]{1,0:T(8,128)(2,1)S(1)}, u32[]{:S(2)}, u32[]{:S(2)}) %collective-permute-start.16) | collective-permute-done | bytes 524320 | tf_op jit(solution)/shard_map/ppermute | solution.py:26
  707.5 7.1 collective-permute-done.17
  717.8 7.1 collective-permute-done.18
  727.2 3.3 collective-permute-done.35
  730.6 10.2 %collective-permute-done.24 = bf16[128,2336]{0,1:T(8,128)(2,1)} collective-permute-done((bf16[128,2336]{0,1:T(8,128)(2,1)S(1)}, bf16[128,2336]{0,1:T(8,128)(2,1)}, u32[]{:S(2)}, u32[]{:S(2)}) %collective-permute-start.24) | collective-permute-done | bytes 598048 | tf_op jit(solution)/shard_map/ppermute | solution.py:26
  745.5 8.9 %collective-permute-done.25 = bf16[64,2336]{1,0:T(8,128)(2,1)S(1)} collective-permute-done((bf16[64,2336]{1,0:T(8,128)(2,1)S(1)}, bf16[64,2336]{1,0:T(8,128)(2,1)S(1)}, u32[]{:S(2)}, u32[]{:S(2)}) %collective-permute-start.25) | collective-permute-done | bytes 299040 | tf_op jit(solution)/shard_map/ppermute | solution.py:26
  756.0 9.6 %collective-permute-done.26 = bf16[32,2336]{1,0:T(8,128)(2,1)S(1)} collective-permute-done((bf16[32,2336]{1,0:T(8,128)(2,1)S(1)}, bf16[32,2336]{1,0:T(8,128)(2,1)S(1)}, u32[]{:S(2)}, u32[]{:S(2)}) %collective-permute-start.26) | collective-permute-done | bytes 149536 | tf_op jit(solution)/shard_map/ppermute | solution.py:26
  765.8 6.9 collective-permute-done.27
  774.5 5.2 collective-permute-done.28
  782.0 6.4 collective-permute-done.21
  789.7 5.1 collective-permute-done.29
  798.9 5.9 copy.286
  (569 shorter events, 157.9 us)
Async XLA Ops:
  2.0 33.9 %copy-start.109 = (bf16[4,576]{1,0:T(4,128)(2,1)S(1)}, bf16[4,576]{1,0:T(4,128)(2,1)}, u32[]{:S(2)}) copy-start(bf16[4,576]{1,0:T(4,128)(2,1)} %param.15) | copy-start | bytes 13828
  2.0 29.5 %collective-permute-start = (bf16[1,256,2336]{1,2,0:T(8,128)(2,1)S(1)}, bf16[1,256,2336]{1,2,0:T(8,128)(2,1)}, u32[]{:S(2)}, u32[]{:S(2)}) collective-permute-start(bf16[1,256,2336]{1,2,0:T(8,128)(2,1)S(1)} %slice_bitcast_fusion), channel_id=1, source_target_pairs={{0,2},{1,3},{2,0},{3,1},{4,6},{5,7},{6,4},{7,5},{8,10},{9,11},{10,... | collective-permute-start | bytes 3588104 | tf_op jit(solution)/shard_map/ppermute | solution.py:26
  5.0 31.3 %copy-start.135 = (u32[32]{0:T(128)S(1)}, u32[32]{0:T(128)}, u32[]{:S(2)}) copy-start(u32[32]{0:T(128)} %constant.282) | copy-start | bytes 388
  5.0 32.5 %copy-start.124 = (bf16[576]{0:T(1024)(128)(2,1)S(1)}, bf16[576]{0:T(1024)(128)(2,1)}, u32[]{:S(2)}) copy-start(bf16[576]{0:T(1024)(128)(2,1)} %param.16) | copy-start | bytes 3460
  5.1 32.5 %copy-start.127 = (bf16[512]{0:T(512)(128)(2,1)S(1)}, bf16[512]{0:T(512)(128)(2,1)}, u32[]{:S(2)}) copy-start(bf16[512]{0:T(512)(128)(2,1)} %param.20) | copy-start | bytes 3076
  5.1 32.5 %copy-start.129 = (bf16[256]{0:T(256)(128)(2,1)S(1)}, bf16[256]{0:T(256)(128)(2,1)}, u32[]{:S(2)}) copy-start(bf16[256]{0:T(256)(128)(2,1)} %param.13) | copy-start | bytes 1540
  5.1 32.5 %copy-start.130 = (bf16[8]{0:T(256)(128)(2,1)S(1)}, bf16[8]{0:T(256)(128)(2,1)}, u32[]{:S(2)}) copy-start(bf16[8]{0:T(256)(128)(2,1)} %param.17) | copy-start | bytes 52
  5.1 32.5 %copy-start.131 = (bf16[8]{0:T(256)(128)(2,1)S(1)}, bf16[8]{0:T(256)(128)(2,1)}, u32[]{:S(2)}) copy-start(bf16[8]{0:T(256)(128)(2,1)} %param.18) | copy-start | bytes 52
  5.1 32.5 %copy-start.132 = (bf16[8]{0:T(256)(128)(2,1)S(1)}, bf16[8]{0:T(256)(128)(2,1)}, u32[]{:S(2)}) copy-start(bf16[8]{0:T(256)(128)(2,1)} %param.19) | copy-start | bytes 52
  35.9 24.1 %collective-permute-start.1 = (bf16[2,256,2336]{1,2,0:T(8,128)(2,1)}, bf16[2,256,2336]{1,2,0:T(8,128)(2,1)}, u32[]{:S(2)}, u32[]{:S(2)}) collective-permute-start(bf16[2,256,2336]{1,2,0:T(8,128)(2,1)} %maximum_bitcast_fusion), channel_id=1, source_target_pairs={{0,1},{1,0},{2,3},{3,2},{4,5},{5,4},{6,7},{7,6},{8,9},{9,8},{10,11... | collective-permute-start | bytes 7176200 | tf_op jit(solution)/shard_map/ppermute | solution.py:26
  51.5 230.2 %copy-start.71 = (f32[1,2,4,128]{3,1,2,0:T(2,128)}, f32[1,2,4,128]{3,1,2,0:T(2,128)S(1)}, u32[]{:S(2)}) copy-start(f32[1,2,4,128]{3,1,2,0:T(2,128)S(1)} %copy.302) | copy-start | bytes 12292
  52.3 27.7 %copy-start.107 = (f32[32]{0:T(128)}, f32[32]{0:T(128)S(1)}, u32[]{:S(2)}) copy-start(f32[32]{0:T(128)S(1)} %add.455) | copy-start | bytes 388
  52.4 27.6 %copy-start.125 = (f32[32]{0:T(128)}, f32[32]{0:T(128)S(1)}, u32[]{:S(2)}) copy-start(f32[32]{0:T(128)S(1)} %neg.28) | copy-start | bytes 388
  58.8 65.7 %copy-start.54 = (f32[2304]{0:T(1024)}, f32[2304]{0:T(1024)S(1)}, u32[]{:S(2)}) copy-start(f32[2304]{0:T(1024)S(1)} %get-tuple-element.100) | copy-start | bytes 27652
  58.8 65.7 %copy-start.56 = (f32[2304]{0:T(1024)}, f32[2304]{0:T(1024)S(1)}, u32[]{:S(2)}) copy-start(f32[2304]{0:T(1024)S(1)} %get-tuple-element.101) | copy-start | bytes 27652
  58.8 65.7 %copy-start.58 = (f32[2304]{0:T(1024)}, f32[2304]{0:T(1024)S(1)}, u32[]{:S(2)}) copy-start(f32[2304]{0:T(1024)S(1)} %get-tuple-element.102) | copy-start | bytes 27652
  58.8 65.7 %copy-start.60 = (f32[2304]{0:T(1024)}, f32[2304]{0:T(1024)S(1)}, u32[]{:S(2)}) copy-start(f32[2304]{0:T(1024)S(1)} %get-tuple-element.103) | copy-start | bytes 27652
  59.3 222.4 %copy-start.73 = (f32[1024]{0:T(1024)}, f32[1024]{0:T(1024)S(1)}, u32[]{:S(2)}) copy-start(f32[1024]{0:T(1024)S(1)} %add_rsqrt_fusion.1) | copy-start | bytes 12292
  60.0 64.5 %copy-start.63 = (f32[1024]{0:T(1024)}, f32[1024]{0:T(1024)S(1)}, u32[]{:S(2)}) copy-start(f32[1024]{0:T(1024)S(1)} %get-tuple-element.226) | copy-start | bytes 12292
  60.0 64.5 %copy-start.65 = (f32[1024]{0:T(1024)}, f32[1024]{0:T(1024)S(1)}, u32[]{:S(2)}) copy-start(f32[1024]{0:T(1024)S(1)} %get-tuple-element.224) | copy-start | bytes 12292
  60.0 64.5 %copy-start.67 = (f32[1024]{0:T(1024)}, f32[1024]{0:T(1024)S(1)}, u32[]{:S(2)}) copy-start(f32[1024]{0:T(1024)S(1)} %get-tuple-element.225) | copy-start | bytes 12292
  60.0 64.5 %copy-start.69 = (f32[1024]{0:T(1024)}, f32[1024]{0:T(1024)S(1)}, u32[]{:S(2)}) copy-start(f32[1024]{0:T(1024)S(1)} %get-tuple-element.229) | copy-start | bytes 12292
  84.7 39.3 %collective-permute-start.2 = (f32[3,2304]{1,0:T(4,128)S(1)}, f32[3,2304]{1,0:T(4,128)S(1)}, u32[]{:S(2)}, u32[]{:S(2)}) collective-permute-start(f32[3,2304]{1,0:T(4,128)S(1)} %copy.250), channel_id=1, source_target_pairs={{0,1},{1,2},{2,3},{4,5},{5,6},{6,7},{8,9},{9,10},{10,11},{12,13},{... | collective-permute-start | bytes 82952 | tf_op jit(solution)/shard_map/ppermute | solution.py:22
  86.9 89.3 %copy-start.82 = (f32[32]{0:T(128)}, f32[32]{0:T(128)S(1)}, u32[]{:S(2)}) copy-start(f32[32]{0:T(128)S(1)} %get-tuple-element.239) | copy-start | bytes 388
  86.9 89.3 %copy-start.84 = (f32[32]{0:T(128)}, f32[32]{0:T(128)S(1)}, u32[]{:S(2)}) copy-start(f32[32]{0:T(128)S(1)} %get-tuple-element.241) | copy-start | bytes 388
  96.1 177.9 %collective-permute-start.8 = (bf16[1,512,1024]{2,1,0:T(8,128)(2,1)}, bf16[1,512,1024]{2,1,0:T(8,128)(2,1)}, u32[]{:S(2)}, u32[]{:S(2)}) collective-permute-start(bf16[1,512,1024]{2,1,0:T(8,128)(2,1)} %bitcast.59), channel_id=1, source_target_pairs={{0,2},{1,3},{2,0},{3,1},{4,6},{5,7},{6,4},{7,5},{8,10},{9,11},{10,... | collective-permute-start | bytes 3145736 | tf_op jit(solution)/shard_map/ppermute | solution.py:26
  97.2 146.0 %collective-permute-start.6 = (bf16[1,256,2048]{2,1,0:T(8,128)(2,1)}, bf16[1,256,2048]{2,1,0:T(8,128)(2,1)}, u32[]{:S(2)}, u32[]{:S(2)}) collective-permute-start(bf16[1,256,2048]{2,1,0:T(8,128)(2,1)} %bitcast.51), channel_id=1, source_target_pairs={{0,2},{1,3},{2,0},{3,1},{4,6},{5,7},{6,4},{7,5},{8,10},{9,11},{10,... | collective-permute-start | bytes 3145736 | tf_op jit(solution)/shard_map/ppermute | solution.py:26
  124.4 24.2 %copy-start.16 = (f32[3,2304]{0,1:T(8,128)}, f32[3,2304]{0,1:T(8,128)S(1)}, u32[]{:S(2)}) copy-start(f32[3,2304]{0,1:T(8,128)S(1)} %copy.251) | copy-start | bytes 82948
  180.1 56.5 %collective-permute-start.5 = (bf16[32,64,128]{2,1,0:T(8,128)(2,1)}, bf16[32,64,128]{2,1,0:T(8,128)(2,1)}, u32[]{:S(2)}, u32[]{:S(2)}) collective-permute-start(bf16[32,64,128]{2,1,0:T(8,128)(2,1)} %get-tuple-element.148), channel_id=1, source_target_pairs={{0,3},{4,7},{8,11},{12,15},{16,19},{20,23},{24,27},{28,31}} | collective-permute-start | bytes 1572872 | tf_op jit(solution)/shard_map/ppermute | solution.py:22
  183.3 53.3 %collective-permute-start.4 = (bf16[32,64,128]{2,1,0:T(8,128)(2,1)}, bf16[32,64,128]{2,1,0:T(8,128)(2,1)}, u32[]{:S(2)}, u32[]{:S(2)}) collective-permute-start(bf16[32,64,128]{2,1,0:T(8,128)(2,1)} %get-tuple-element.148), channel_id=1, source_target_pairs={{0,2},{1,3},{4,6},{5,7},{8,10},{9,11},{12,14},{13,15},{16,18},{17,... | collective-permute-start | bytes 1572872 | tf_op jit(solution)/shard_map/ppermute | solution.py:22
  185.4 51.2 %collective-permute-start.3 = (bf16[32,64,128]{2,1,0:T(8,128)(2,1)}, bf16[32,64,128]{2,1,0:T(8,128)(2,1)}, u32[]{:S(2)}, u32[]{:S(2)}) collective-permute-start(bf16[32,64,128]{2,1,0:T(8,128)(2,1)} %get-tuple-element.148), channel_id=1, source_target_pairs={{0,1},{1,2},{2,3},{4,5},{5,6},{6,7},{8,9},{9,10},{10,11},{12,13},{... | collective-permute-start | bytes 1572872 | tf_op jit(solution)/shard_map/ppermute | solution.py:22
  248.5 28.7 %collective-permute-start.7 = (bf16[2,256,2048]{2,1,0:T(8,128)(2,1)}, bf16[2,256,2048]{2,1,0:T(8,128)(2,1)}, u32[]{:S(2)}, u32[]{:S(2)}) collective-permute-start(bf16[2,256,2048]{2,1,0:T(8,128)(2,1)} %maximum_bitcast_fusion.1), channel_id=1, source_target_pairs={{0,1},{1,0},{2,3},{3,2},{4,5},{5,4},{6,7},{7,6},{8,9},{9,8},{10,11... | collective-permute-start | bytes 6291464 | tf_op jit(solution)/shard_map/ppermute | solution.py:26
  277.2 16.9 %collective-permute-start.9 = (bf16[2,512,1024]{2,1,0:T(8,128)(2,1)}, bf16[2,512,1024]{2,1,0:T(8,128)(2,1)}, u32[]{:S(2)}, u32[]{:S(2)}) collective-permute-start(bf16[2,512,1024]{2,1,0:T(8,128)(2,1)} %maximum_bitcast_fusion.2), channel_id=1, source_target_pairs={{0,1},{1,0},{2,3},{3,2},{4,5},{5,4},{6,7},{7,6},{8,9},{9,8},{10,11... | collective-permute-start | bytes 6291464 | tf_op jit(solution)/shard_map/ppermute | solution.py:26
  305.5 23.8 %slice-start = ((s8[8388608]{0:T(1024)(128)(4,1)}), s8[4194304]{0:T(1024)(128)(4,1)S(1)}, s32[]{:S(2)}) async-start(s8[8388608]{0:T(1024)(128)(4,1)} %bitcast.412), calls=%async_computation | async-start | bytes 8388608
  377.8 50.3 %collective-permute-start.12 = (bf16[32,64,128]{2,1,0:T(8,128)(2,1)}, bf16[32,64,128]{2,1,0:T(8,128)(2,1)}, u32[]{:S(2)}, u32[]{:S(2)}) collective-permute-start(bf16[32,64,128]{2,1,0:T(8,128)(2,1)} %get-tuple-element.134), channel_id=1, source_target_pairs={{3,0},{7,4},{11,8},{15,12},{19,16},{23,20},{27,24},{31,28}} | collective-permute-start | bytes 1572872 | tf_op jit(solution)/shard_map/ppermute | solution.py:22
  379.1 49.0 %collective-permute-start.11 = (bf16[32,64,128]{2,1,0:T(8,128)(2,1)}, bf16[32,64,128]{2,1,0:T(8,128)(2,1)}, u32[]{:S(2)}, u32[]{:S(2)}) collective-permute-start(bf16[32,64,128]{2,1,0:T(8,128)(2,1)} %get-tuple-element.134), channel_id=1, source_target_pairs={{2,0},{3,1},{6,4},{7,5},{10,8},{11,9},{14,12},{15,13},{18,16},{19,... | collective-permute-start | bytes 1572872 | tf_op jit(solution)/shard_map/ppermute | solution.py:22
  380.4 47.7 %collective-permute-start.10 = (bf16[32,64,128]{2,1,0:T(8,128)(2,1)}, bf16[32,64,128]{2,1,0:T(8,128)(2,1)}, u32[]{:S(2)}, u32[]{:S(2)}) collective-permute-start(bf16[32,64,128]{2,1,0:T(8,128)(2,1)} %get-tuple-element.134), channel_id=1, source_target_pairs={{1,0},{2,1},{3,2},{5,4},{6,5},{7,6},{9,8},{10,9},{11,10},{13,12},{... | collective-permute-start | bytes 1572872 | tf_op jit(solution)/shard_map/ppermute | solution.py:22
  416.7 222.0 %collective-permute-start.30 = (bf16[2,512,1024]{2,1,0:T(8,128)(2,1)}, bf16[2,512,1024]{2,1,0:T(8,128)(2,1)}, u32[]{:S(2)}, u32[]{:S(2)}) collective-permute-start(bf16[2,512,1024]{2,1,0:T(8,128)(2,1)} %fusion.49), channel_id=1, source_target_pairs={{0,1},{1,0},{2,3},{3,2},{4,5},{5,4},{6,7},{7,6},{8,9},{9,8},{10,11... | collective-permute-start | bytes 6291464 | tf_op jit(solution)/shard_map/ppermute | solution.py:26
  427.1 216.9 %collective-permute-start.14 = (bf16[2,256,2048]{2,1,0:T(8,128)(2,1)}, bf16[2,256,2048]{2,1,0:T(8,128)(2,1)}, u32[]{:S(2)}, u32[]{:S(2)}) collective-permute-start(bf16[2,256,2048]{2,1,0:T(8,128)(2,1)} %fusion.48), channel_id=1, source_target_pairs={{0,1},{1,0},{2,3},{3,2},{4,5},{5,4},{6,7},{7,6},{8,9},{9,8},{10,11... | collective-permute-start | bytes 6291464 | tf_op jit(solution)/shard_map/ppermute | solution.py:26
  467.9 20.0 %slice-start.2 = ((s8[9437184]{0:T(1024)(128)(4,1)}), s8[4194304]{0:T(1024)(128)(4,1)S(1)}, s32[]{:S(2)}) async-start(s8[9437184]{0:T(1024)(128)(4,1)} %bitcast.414), calls=%async_computation.2 | async-start | bytes 8388608
  468.0 20.0 %slice-start.3 = ((s8[9437184]{0:T(1024)(128)(4,1)}), s8[4194304]{0:T(1024)(128)(4,1)S(1)}, s32[]{:S(2)}) async-start(s8[9437184]{0:T(1024)(128)(4,1)} %bitcast.414), calls=%async_computation.3 | async-start | bytes 8388608
  508.8 3.4 collective-permute-start.13
  629.0 17.8 %collective-permute-start.22 = (bf16[2,256,2336]{1,2,0:T(8,128)(2,1)}, bf16[2,256,2336]{1,2,0:T(8,128)(2,1)}, u32[]{:S(2)}, u32[]{:S(2)}) collective-permute-start(bf16[2,256,2336]{1,2,0:T(8,128)(2,1)} %bitcast.391), channel_id=1, source_target_pairs={{0,1},{1,0},{2,3},{3,2},{4,5},{5,4},{6,7},{7,6},{8,9},{9,8},{10,11... | collective-permute-start | bytes 7176200 | tf_op jit(solution)/shard_map/ppermute | solution.py:26
  641.7 26.3 %collective-permute-start.31 = (bf16[1,512,1024]{2,1,0:T(8,128)(2,1)S(1)}, bf16[1,512,1024]{2,1,0:T(8,128)(2,1)S(1)}, u32[]{:S(2)}, u32[]{:S(2)}) collective-permute-start(bf16[1,512,1024]{2,1,0:T(8,128)(2,1)S(1)} %dynamic-slice_convert_fusion.1), channel_id=1, source_target_pairs={{0,2},{1,3},{2,0},{3,1},{4,6},{5,7},{6,4},{7,5},{8,10},{9,11},{10,... | collective-permute-start | bytes 3145736 | tf_op jit(solution)/shard_map/ppermute | solution.py:26
  646.7 43.6 %collective-permute-start.15 = (bf16[1,256,2048]{2,1,0:T(8,128)(2,1)S(1)}, bf16[1,256,2048]{2,1,0:T(8,128)(2,1)S(1)}, u32[]{:S(2)}, u32[]{:S(2)}) collective-permute-start(bf16[1,256,2048]{2,1,0:T(8,128)(2,1)S(1)} %dynamic-slice_convert_fusion.2), channel_id=1, source_target_pairs={{0,2},{1,3},{2,0},{3,1},{4,6},{5,7},{6,4},{7,5},{8,10},{9,11},{10,... | collective-permute-start | bytes 3145736 | tf_op jit(solution)/shard_map/ppermute | solution.py:26
  668.4 24.7 %collective-permute-start.32 = (bf16[256,1024]{1,0:T(8,128)(2,1)S(1)}, bf16[256,1024]{1,0:T(8,128)(2,1)S(1)}, u32[]{:S(2)}, u32[]{:S(2)}) collective-permute-start(bf16[256,1024]{1,0:T(8,128)(2,1)S(1)} %fusion.55), channel_id=1, source_target_pairs={{0,4},{4,0},{8,12},{12,8},{16,20},{20,16},{24,28},{28,24},{1,5},{5... | collective-permute-start | bytes 1572872 | tf_op jit(solution)/shard_map/ppermute | solution.py:26
  690.6 13.8 %collective-permute-start.16 = (bf16[128,2048]{1,0:T(8,128)(2,1)S(1)}, bf16[128,2048]{1,0:T(8,128)(2,1)S(1)}, u32[]{:S(2)}, u32[]{:S(2)}) collective-permute-start(bf16[128,2048]{1,0:T(8,128)(2,1)S(1)} %fusion.54), channel_id=1, source_target_pairs={{0,4},{4,0},{8,12},{12,8},{16,20},{20,16},{24,28},{28,24},{1,5},{5... | collective-permute-start | bytes 1572872 | tf_op jit(solution)/shard_map/ppermute | solution.py:26
  692.5 32.5 %collective-permute-start.23 = (bf16[1,256,2336]{1,2,0:T(8,128)(2,1)S(1)}, bf16[1,256,2336]{1,2,0:T(8,128)(2,1)S(1)}, u32[]{:S(2)}, u32[]{:S(2)}) collective-permute-start(bf16[1,256,2336]{1,2,0:T(8,128)(2,1)S(1)} %dynamic-slice_convert_fusion), channel_id=1, source_target_pairs={{0,2},{1,3},{2,0},{3,1},{4,6},{5,7},{6,4},{7,5},{8,10},{9,11},{10,... | collective-permute-start | bytes 3588104 | tf_op jit(solution)/shard_map/ppermute | solution.py:26
  693.3 12.8 %collective-permute-start.33 = (bf16[128,1024]{1,0:T(8,128)(2,1)S(1)}, bf16[128,1024]{1,0:T(8,128)(2,1)S(1)}, u32[]{:S(2)}, u32[]{:S(2)}) collective-permute-start(bf16[128,1024]{1,0:T(8,128)(2,1)S(1)} %dynamic-slice_convert_fusion.7), channel_id=1, source_target_pairs={{0,8},{4,12},{8,0},{12,4},{16,24},{20,28},{24,16},{28,20},{1,9},{5... | collective-permute-start | bytes 786440 | tf_op jit(solution)/shard_map/ppermute | solution.py:26
  704.5 10.1 %collective-permute-start.17 = (bf16[64,2048]{1,0:T(8,128)(2,1)S(1)}, bf16[64,2048]{1,0:T(8,128)(2,1)S(1)}, u32[]{:S(2)}, u32[]{:S(2)}) collective-permute-start(bf16[64,2048]{1,0:T(8,128)(2,1)S(1)} %dynamic-slice_convert_fusion.8), channel_id=1, source_target_pairs={{0,8},{4,12},{8,0},{12,4},{16,24},{20,28},{24,16},{28,20},{1,9},{5... | collective-permute-start | bytes 786440 | tf_op jit(solution)/shard_map/ppermute | solution.py:26
  706.2 9.5 %collective-permute-start.34 = (bf16[64,1024]{1,0:T(8,128)(2,1)S(1)}, bf16[64,1024]{1,0:T(8,128)(2,1)S(1)}, u32[]{:S(2)}, u32[]{:S(2)}) collective-permute-start(bf16[64,1024]{1,0:T(8,128)(2,1)S(1)} %dynamic-slice_convert_fusion.10), channel_id=1, source_target_pairs={{0,16},{4,20},{8,24},{12,28},{16,0},{20,4},{24,8},{28,12},{1,17},{... | collective-permute-start | bytes 393224 | tf_op jit(solution)/shard_map/ppermute | solution.py:26
  714.7 10.2 %collective-permute-start.18 = (bf16[32,2048]{1,0:T(8,128)(2,1)S(1)}, bf16[32,2048]{1,0:T(8,128)(2,1)S(1)}, u32[]{:S(2)}, u32[]{:S(2)}) collective-permute-start(bf16[32,2048]{1,0:T(8,128)(2,1)S(1)} %dynamic-slice_convert_fusion.11), channel_id=1, source_target_pairs={{0,16},{4,20},{8,24},{12,28},{16,0},{20,4},{24,8},{28,12},{1,17},{... | collective-permute-start | bytes 393224 | tf_op jit(solution)/shard_map/ppermute | solution.py:26
  715.8 14.7 %collective-permute-start.35 = (bf16[64,1024]{1,0:T(8,128)(2,1)S(1)}, bf16[64,1024]{1,0:T(8,128)(2,1)S(1)}, u32[]{:S(2)}, u32[]{:S(2)}) collective-permute-start(bf16[64,1024]{1,0:T(8,128)(2,1)S(1)} %add_convert_fusion.3), channel_id=1, source_target_pairs={{0,16},{4,20},{8,24},{12,28},{16,0},{20,4},{24,8},{28,12},{1,17},{... | collective-permute-start | bytes 393224 | tf_op jit(solution)/shard_map/ppermute | solution.py:26
  724.9 18.9 %collective-permute-start.19 = (bf16[32,2048]{1,0:T(8,128)(2,1)S(1)}, bf16[32,2048]{1,0:T(8,128)(2,1)}, u32[]{:S(2)}, u32[]{:S(2)}) collective-permute-start(bf16[32,2048]{1,0:T(8,128)(2,1)S(1)} %add_convert_fusion.4), channel_id=1, source_target_pairs={{0,16},{4,20},{8,24},{12,28},{16,0},{20,4},{24,8},{28,12},{1,17},{... | collective-permute-start | bytes 393224 | tf_op jit(solution)/shard_map/ppermute | solution.py:26
  725.3 15.5 %collective-permute-start.24 = (bf16[128,2336]{0,1:T(8,128)(2,1)S(1)}, bf16[128,2336]{0,1:T(8,128)(2,1)}, u32[]{:S(2)}, u32[]{:S(2)}) collective-permute-start(bf16[128,2336]{0,1:T(8,128)(2,1)S(1)} %fusion.53), channel_id=1, source_target_pairs={{0,4},{4,0},{8,12},{12,8},{16,20},{20,16},{24,28},{28,24},{1,5},{5... | collective-permute-start | bytes 1794056 | tf_op jit(solution)/shard_map/ppermute | solution.py:26
  730.5 25.0 %collective-permute-start.36 = (bf16[128,1024]{1,0:T(8,128)(2,1)S(1)}, bf16[128,1024]{1,0:T(8,128)(2,1)S(1)}, u32[]{:S(2)}, u32[]{:S(2)}) collective-permute-start(bf16[128,1024]{1,0:T(8,128)(2,1)S(1)} %pad_maximum_fusion.13), channel_id=1, source_target_pairs={{0,8},{4,12},{8,0},{12,4},{16,24},{20,28},{24,16},{28,20},{1,9},{5... | collective-permute-start | bytes 786440 | tf_op jit(solution)/shard_map/ppermute | solution.py:26
  742.4 12.0 %collective-permute-start.25 = (bf16[64,2336]{1,0:T(8,128)(2,1)S(1)}, bf16[64,2336]{1,0:T(8,128)(2,1)S(1)}, u32[]{:S(2)}, u32[]{:S(2)}) collective-permute-start(bf16[64,2336]{1,0:T(8,128)(2,1)S(1)} %dynamic-slice_convert_fusion.6), channel_id=1, source_target_pairs={{0,8},{4,12},{8,0},{12,4},{16,24},{20,28},{24,16},{28,20},{1,9},{5... | collective-permute-start | bytes 897032 | tf_op jit(solution)/shard_map/ppermute | solution.py:26
  744.8 20.9 %collective-permute-start.20 = (bf16[64,2048]{1,0:T(8,128)(2,1)S(1)}, bf16[64,2048]{1,0:T(8,128)(2,1)S(1)}, u32[]{:S(2)}, u32[]{:S(2)}) collective-permute-start(bf16[64,2048]{1,0:T(8,128)(2,1)S(1)} %pad_maximum_fusion.12), channel_id=1, source_target_pairs={{0,8},{4,12},{8,0},{12,4},{16,24},{20,28},{24,16},{28,20},{1,9},{5... | collective-permute-start | bytes 786440 | tf_op jit(solution)/shard_map/ppermute | solution.py:26
  754.5 11.1 %collective-permute-start.26 = (bf16[32,2336]{1,0:T(8,128)(2,1)S(1)}, bf16[32,2336]{1,0:T(8,128)(2,1)S(1)}, u32[]{:S(2)}, u32[]{:S(2)}) collective-permute-start(bf16[32,2336]{1,0:T(8,128)(2,1)S(1)} %dynamic-slice_convert_fusion.9), channel_id=1, source_target_pairs={{0,16},{4,20},{8,24},{12,28},{16,0},{20,4},{24,8},{28,12},{1,17},{... | collective-permute-start | bytes 448520 | tf_op jit(solution)/shard_map/ppermute | solution.py:26
  755.7 18.6 %collective-permute-start.37 = (bf16[256,1024]{1,0:T(8,128)(2,1)S(1)}, bf16[256,1024]{1,0:T(8,128)(2,1)S(1)}, u32[]{:S(2)}, u32[]{:S(2)}) collective-permute-start(bf16[256,1024]{1,0:T(8,128)(2,1)S(1)} %pad_maximum_fusion.10), channel_id=1, source_target_pairs={{0,4},{4,0},{8,12},{12,8},{16,20},{20,16},{24,28},{28,24},{1,5},{5... | collective-permute-start | bytes 1572872 | tf_op jit(solution)/shard_map/ppermute | solution.py:26
  765.6 7.1 collective-permute-start.27
  772.8 7.0 collective-permute-start.28
  773.7 14.7 %collective-permute-start.21 = (bf16[128,2048]{1,0:T(8,128)(2,1)}, bf16[128,2048]{1,0:T(8,128)(2,1)}, u32[]{:S(2)}, u32[]{:S(2)}) collective-permute-start(bf16[128,2048]{1,0:T(8,128)(2,1)} %pad_maximum_fusion.9), channel_id=1, source_target_pairs={{0,4},{4,0},{8,12},{12,8},{16,20},{20,16},{24,28},{28,24},{1,5},{5... | collective-permute-start | bytes 1572872 | tf_op jit(solution)/shard_map/ppermute | solution.py:26
  780.2 14.6 %collective-permute-start.29 = (bf16[128,2336]{0,1:T(8,128)(2,1)S(1)}, bf16[128,2336]{0,1:T(8,128)(2,1)}, u32[]{:S(2)}, u32[]{:S(2)}) collective-permute-start(bf16[128,2336]{0,1:T(8,128)(2,1)S(1)} %copy.282), channel_id=1, source_target_pairs={{0,4},{4,0},{8,12},{12,8},{16,20},{20,16},{24,28},{28,24},{1,5},{5... | collective-permute-start | bytes 1794056 | tf_op jit(solution)/shard_map/ppermute | solution.py:26
  (130 other events, 788.1 us)

commit v2 on v1

--- a/solution.py
+++ b/solution.py
@@ -1,6 +1,7 @@
 import jax
 import jax.numpy as jnp
 from jax import lax
+from jax.experimental.layout import Layout, with_layout_constraint
 from jax.sharding import PartitionSpec as P
 
 H = 32
@@ -20,6 +21,10 @@
     peers = lax.axis_size(axis)
     pairs = [(i, i + by) for i in range(peers) if 0 <= i + by < peers]
     return lax.ppermute(x, axis, pairs)
+
+
+def pinned(v):
+    return with_layout_constraint(v, Layout(major_to_minor=tuple(range(v.ndim))))
 
 
 def swapped(x, axis, bit):
@@ -49,36 +54,88 @@
     return held.reshape((count * x.shape[0],) + x.shape[1:])
 
 
-def reduce_rows(partial):
+def owner_stages(held):
     owners, mine = lax.axis_size("fsdp"), lax.axis_index("fsdp")
-    held = partial.reshape((owners, partial.shape[0] // owners) + partial.shape[1:])
     bit = 1
     while bit < owners:
         pair = held.reshape((held.shape[0] // 2, 2) + held.shape[1:])
         side = (mine // bit) % 2
         keep = lax.dynamic_index_in_dim(pair, side, 1, False)
         send = lax.dynamic_index_in_dim(pair, 1 - side, 1, False).astype(low)
-        held = keep + swapped(send, "fsdp", bit).astype(wide)
+        held = yield keep + swapped(send, "fsdp", bit).astype(wide)
         bit *= 2
-    held = held[0]
-    copies, here = lax.axis_size("rep"), lax.axis_index("rep")
-    bit = 1
-    while bit < copies:
+    return held[0]
+
+
+def rep_bits(last_first):
+    bits, bit = [], 1
+    while bit < lax.axis_size("rep"):
+        bits.append(bit)
+        bit *= 2
+    return bits[1:] + bits[:1] if last_first else bits
+
+
+def sum_stages(partial, last_first):
+    owners = lax.axis_size("fsdp")
+    held = partial.reshape((owners, partial.shape[0] // owners) + partial.shape[1:])
+    held = yield from owner_stages(held)
+    here, bits = lax.axis_index("rep"), rep_bits(last_first)
+    for bit in bits:
         half = held.shape[0] // 2
         side = (here // bit) % 2
         keep = lax.dynamic_slice_in_dim(held, side * half, half, 0)
         send = lax.dynamic_slice_in_dim(held, (1 - side) * half, half, 0).astype(low)
-        held = keep + swapped(send, "rep", bit).astype(wide)
-        bit *= 2
+        held = yield keep + swapped(send, "rep", bit).astype(wide)
     held = held.astype(low)
-    while bit > 1:
-        bit //= 2
+    for bit in reversed(bits):
         other = swapped(held, "rep", bit)
         lower = ((here // bit) % 2) == 0
-        held = jnp.concatenate(
+        held = yield jnp.concatenate(
             [jnp.where(lower, held, other), jnp.where(lower, other, held)], axis=0
         )
-    return held.astype(wide)
+
+
+class Reduction:
+    def __init__(self, partial, last_first=False):
+        self.stages = sum_stages(partial, last_first)
+        self.value = next(self.stages)
+        self.done = False
+
+    def advance(self):
+        if not self.done:
+            try:
+                self.value = self.stages.send(self.value)
+            except StopIteration:
+                self.done = True
+
+    def finish(self):
+        while not self.done:
+            self.advance()
+        return self.value.astype(wide)
+
+
+def beside(value, *running):
+    tied = lax.optimization_barrier((value,) + tuple(r.value for r in running))
+    for r, held in zip(running, tied[1:]):
+        r.value = held
+        r.advance()
+    return tied[0]
+
+
+def sum_small(held):
+    owners, mine = lax.axis_size("fsdp"), lax.axis_index("fsdp")
+    bit = 1
+    while bit < owners:
+        pair = held.reshape((held.shape[0] // 2, 2) + held.shape[1:])
+        side = (mine // bit) % 2
+        keep = lax.dynamic_index_in_dim(pair, side, 1, False)
+        send = lax.dynamic_index_in_dim(pair, 1 - side, 1, False)
+        held = keep + swapped(send, "fsdp", bit)
+        bit *= 2
+    held = held[0]
+    for bit in rep_bits(False):
+        held = held + swapped(held, "rep", bit)
+    return held
 
 
 def silu_parts(x):
@@ -104,16 +161,19 @@
     length = tokens.shape[0]
     count = length // CHUNK
     taps = conv_w.shape[0]
-    smalls = (norm_w, conv_w.T, conv_b, dt_bias, a_log, d_skip, gnorm_w)
-    flat = lax.all_gather(jnp.concatenate([v.reshape(-1) for v in smalls]), "fsdp", axis=0)
+    mixed = E + 2 * N
+    in_dt = in_w[:, E + mixed :]
+    smalls = (norm_w, conv_w.T, conv_b, dt_bias, a_log, d_skip, gnorm_w, in_dt)
+    flat = gather_rows(jnp.concatenate([v.reshape(-1) for v in smalls])[None], "fsdp")
     flat = flat.astype(wide)
     parts, at = [], 0
     for v in smalls:
         parts.append(flat[:, at : at + v.size].reshape((ranks * v.shape[0],) + v.shape[1:]))
         at += v.size
-    norm32, conv32, bias32, dt32, alog32, skip32, gnorm32 = parts
+    norm32, conv32, bias32, dt32, alog32, skip32, gnorm32, w_dt = parts
+    w_dt = w_dt.astype(low)
     conv32 = conv32.T
-    w_x = gather_rows(in_w[:, E:], "fsdp")
+    w_x = gather_rows(in_w[:, E : E + mixed], "fsdp")
     in_z, out_s, w_x = lax.optimization_barrier((in_w[:, :E], out_w, w_x))
     w_z = gather_rows(in_z, "fsdp")
     w_out = gather_rows(out_s, "fsdp")
@@ -130,8 +190,7 @@
     u = tokens.astype(wide)
     scale_in = lax.rsqrt(jnp.mean(u * u, axis=-1, keepdims=True) + epsilon)
     normed = (u * scale_in * norm32[None, :]).astype(low)
-    proj_x = jnp.dot(normed, w_x, preferred_element_type=wide)
-    xbc = proj_x[:, : E + 2 * N]
+    xbc = jnp.dot(normed, w_x, preferred_element_type=wide)
     rim = shifted(xbc[length - (taps - 1) :], "fsdp", 1)
 
     full = jnp.concatenate([rim, xbc], axis=0)
@@ -140,7 +199,7 @@
         pre = pre + full[k : k + length] * conv32[k][None, :] * tap_valid(k, 0, length)
     xc = pre * jax.nn.sigmoid(pre)
 
-    draw = proj_x[:, E + 2 * N :] + dt32[None, :]
+    draw = jnp.dot(normed, w_dt, preferred_element_type=wide) + dt32[None, :]
     delta_rows = jax.nn.softplus(draw)
     reset = RESET * (places[:length] == boundary).astype(wide)
     rate = -jnp.exp(alog32)
@@ -155,7 +214,7 @@
     cum = exact("chs,st->cht", decay, upto)
     last = cum[:, :, -1]
     growth = jnp.exp(last)
-    totals = lax.all_gather(jnp.exp(jnp.sum(last, axis=0)), "fsdp", axis=0)
+    own_total = jnp.exp(jnp.sum(last, axis=0))
     entry = jnp.exp(cum)[:, :, None, :]
     tail = jnp.exp(last[:, :, None] - cum)[:, :, None, :]
 
@@ -171,12 +230,12 @@
     def turned_back(v):
         return flatten(v).transpose(0, 2, 1).reshape(length, E)
 
-    x = turned(xc[:, :E])
+    x = pinned(turned(xc[:, :E]))
     bmat = xc[:, E : E + N].reshape(count, CHUNK, N)
     cmat = xc[:, E + N :].reshape(count, CHUNK, N)
     xd = x * delta[:, :, None, :]
     xd_low = xd.astype(low)
-    xw = (xd * tail).astype(low)
+    xw = pinned((xd * tail).astype(low))
     state_own = mm("ceq,cqn->cen", flatten(xw), bmat).reshape(count, H, P_SIZE, N)
 
     def widen(v):
@@ -194,8 +253,8 @@
         for j in range(1, ranks):
             got = shifted(value, "fsdp", sign * j).astype(wide)
             total = total + got * widen(factor)
-            source = jnp.clip(rank - sign * j, 0, ranks - 1)
-            factor = factor * lax.dynamic_index_in_dim(totals, source, 0, False)
+            if j < ranks - 1:
+                factor = factor * shifted(own_total, "fsdp", sign * j)
         return total
 
     inflow = incoming(final, 1)
@@ -213,7 +272,7 @@
         + from_state
         + x * skip32[None, :, None, None]
     )
-    y = turned_back(y_t)
+    y = turned_back(pinned(y_t))
 
     z = jnp.dot(normed, w_z, preferred_element_type=wide)
     silu_z, slope_z = silu_parts(z)
@@ -224,18 +283,20 @@
     output = (u + jnp.dot(gated, w_out, preferred_element_type=wide)).astype(low)
 
     d_gated = jnp.dot(cotangent, w_out.T, preferred_element_type=wide)
-    d_out_w = reduce_rows(mm("te,td->ed", gated, cotangent))
+    sum_out = Reduction(mm("te,td->ed", gated, cotangent))
     d_gnorm = jnp.sum(d_gated * hat, axis=0)
     d_hat = d_gated * gnorm32[None, :]
     d_g = scale_g * (d_hat - hat * jnp.mean(d_hat * hat, axis=-1, keepdims=True))
     d_y = d_g * silu_z
     d_z = (d_g * y * slope_z).astype(low)
-    d_in_z = reduce_rows(mm("td,te->de", normed, d_z))
-
-    dy = turned(d_y)
+    sum_z = Reduction(mm("td,te->de", normed, d_z), True)
+    d_y = beside(d_y, sum_out)
+
+    dy = pinned(turned(d_y))
+    dy = beside(dy, sum_z)
     dy_low = dy.astype(low)
     d_skip_own = jnp.sum(x * dy, axis=(0, 2, 3))
-    faded = (dy * entry).astype(low)
+    faded = pinned((dy * entry).astype(low))
     direct = mm("cet,ctn->cen", flatten(faded), cmat).reshape(count, H, P_SIZE, N)
     leaving = [None] * count + [jnp.zeros((H, P_SIZE, N), wide)]
     after = [None] * count + [jnp.ones((H,), wide)]
@@ -246,12 +307,15 @@
     d_state = jnp.stack([leaving[c + 1] + outflow * widen(after[c + 1]) for c in range(count)])
     d_state_low = d_state.astype(low).reshape(count, E, N)
 
+    dy_low = beside(dy_low, sum_out)
     d_mix = mm("chpt,chps->chts", dy_low, xd_low) * fade
     d_inner = jnp.sum(d_mix, axis=1)
     weight = d_mix * inner[:, None]
     d_cum = jnp.sum(weight, axis=3) - jnp.sum(weight, axis=2) + jnp.sum(dy * from_state, axis=2)
+    d_cum = beside(d_cum, sum_out, sum_z)
     pulled = heads(mm("cen,cqn->ceq", d_state_low, bmat)) * tail
     d_xd = mm("chts,chpt->chps", mixing, dy_low) + pulled
+    d_xd = beside(d_xd, sum_out, sum_z)
     d_tail = jnp.sum(xd * pulled, axis=2)
     d_keep = growth * jnp.sum(state * d_state, axis=(2, 3))
     d_decay = (
@@ -261,7 +325,10 @@
     )
     d_delta = jnp.sum(x * d_xd, axis=2) + d_decay * rate[None, :, None]
     d_alog = jnp.sum(d_decay * delta, axis=(0, 2)) * rate
-    d_x = turned_back(d_xd * delta[:, :, None, :] + dy * skip32[None, :, None, None])
+    d_x = turned_back(
+        pinned(d_xd * delta[:, :, None, :] + dy * skip32[None, :, None, None])
+    )
+    d_x = beside(d_x, sum_out, sum_z)
     d_c = mm("cts,csn->ctn", d_inner, bmat) + mm("cet,cen->ctn", flatten(faded), state_low)
     d_b = mm("cts,ctn->csn", d_inner, cmat) + mm("ceq,cen->cqn", flatten(xw), d_state_low)
     d_draw = d_delta.transpose(0, 2, 1).reshape(length, H) * jax.nn.sigmoid(draw)
@@ -269,6 +336,7 @@
 
     d_xc = jnp.concatenate([d_x, d_b.reshape(length, N), d_c.reshape(length, N)], axis=1)
     d_pre = d_xc * silu_parts(pre)[1]
+    d_pre = beside(d_pre, sum_out, sum_z)
     d_rim = shifted(d_pre[: taps - 1], "fsdp", -1)
     d_bias = jnp.sum(d_pre, axis=0)
     d_conv = jnp.stack(
@@ -284,9 +352,15 @@
         d_xbc = d_xbc + d_full[lo : lo + length] * conv32[k][None, :] * tap_valid(
             k, lo, lo + length
         )
-    d_proj_x = jnp.concatenate([d_xbc.astype(low), d_draw.astype(low)], axis=1)
-    d_in_x = reduce_rows(mm("td,te->de", normed, d_proj_x))
-    d_normed = mm("te,de->td", d_z, w_z) + mm("te,de->td", d_proj_x, w_x)
+    d_xbc = beside(d_xbc.astype(low), sum_out, sum_z)
+    middle = mixed // 2
+    sum_a = Reduction(mm("td,te->de", normed, d_xbc[:, :middle]))
+    sum_b = Reduction(mm("td,te->de", normed, d_xbc[:, middle:]), True)
+    draw_low = d_draw.astype(low)
+    d_in_dt = mm("td,te->de", normed, draw_low)
+    d_normed = mm("te,de->td", d_z, w_z)
+    d_xbc, d_normed = beside((d_xbc, d_normed), sum_a, sum_b)
+    d_normed = d_normed + mm("te,de->td", d_xbc, w_x) + mm("te,de->td", draw_low, w_dt)
     hat_in = u * scale_in
     d_norm = jnp.sum(d_normed * hat_in, axis=0)
     d_hat_in = d_normed * norm32[None, :]
@@ -294,27 +368,28 @@
         d_hat_in - hat_in * jnp.mean(d_hat_in * hat_in, axis=-1, keepdims=True)
     )
 
-    owned = (d_norm, d_conv.T, d_bias, d_dt, d_alog, d_skip_own, d_gnorm)
+    owned = (d_norm, d_conv.T, d_bias, d_dt, d_alog, d_skip_own, d_gnorm, d_in_dt)
     stacked = jnp.concatenate([v.reshape(ranks, -1) for v in owned], axis=1)
-    summed = lax.psum(stacked, ("rep", "fsdp"))
-    mine = lax.dynamic_index_in_dim(summed, rank, 0, False)
+    mine = sum_small(stacked)
     grads, at = [], 0
     for v in smalls:
         grads.append(mine[at : at + v.size].reshape(v.shape))
         at += v.size
-    g_norm, g_conv, g_bias, g_dt, g_alog, g_skip, g_gnorm = grads
+    g_norm, g_conv, g_bias, g_dt, g_alog, g_skip, g_gnorm, g_in_dt = grads
     return (
         output,
         d_tokens,
         g_norm,
-        jnp.concatenate([d_in_z, d_in_x], axis=1),
+        jnp.concatenate(
+            [sum_z.finish(), sum_a.finish(), sum_b.finish(), g_in_dt], axis=1
+        ),
         g_conv.T,
         g_bias,
         g_dt,
         g_alog,
         g_skip,
         g_gnorm,
-        d_out_w,
+        sum_out.finish(),
     )
 
 

time: 817 us -> 791 us (0.968)
  blocking collectives: 78.4 us -> 0 us
  waiting for transfers between devices: 145 us -> 215 us
  local copies, waits for them, and re-layouts: 203 us -> 157 us
  starting transfers between devices: 41.3 us -> 63.6 us
  other arithmetic: 193 us -> 207 us
  matrix products: 139 us -> 128 us
    ppermute x30 -> x45, waiting for transfers between devices: 145 us -> 208 us  [swapped(): lax.ppermute(x, axis, [(i, i ^ bit) for i in range(lax.axis_size(axis))])]
    psum x1 -> x0, blocking collectives: 44.7 us -> none  [body(): summed = lax.psum(stacked, ('rep', 'fsdp'))]
    mul x6 -> x0, local copies, waits for them, and re-layouts: 38.7 us -> none  [the longest x2 12.9 us: body(): xw = (xd * tail).astype(low)]
    unnamed x2 -> x0, blocking collectives: 33.7 us -> none
    reshape x11 -> x0, local copies, waits for them, and re-layouts: 17.8 us -> none  [the longest x1 11 us: flatten(): return v.reshape(count, E, CHUNK)]
    transpose x4 -> x2, local copies, waits for them, and re-layouts: 18.8 us -> 1.26 us  [the longest x1 0.87 us: body(): smalls = (norm_w, conv_w.T, conv_b, dt_bias, a_log, d_skip, gnorm_w, in_dt)]
    add x12 -> x24, other arithmetic: 8.77 us -> 26.3 us  [the longest x8 22 us: owner_stages(): held = (yield (keep + swapped(send, 'fsdp', bit).astype(wide)))]
    convert_element_type x7 -> x9, other arithmetic: 42.2 us -> 26 us  [the longest x1 17.3 us: body(): d_xbc = beside(d_xbc.astype(low), sum_out, sum_z)]
  transfers between devices with their start and end apart: 38 -> 57, of which waited for: 14 -> 27; matrix products, arithmetic and copies ran while one was open for 50% -> 38% of each run, Pallas kernels for 0% -> 0%
where the time goes in v2:
time: 791 us; the launch traced here: 776 us
  waiting for transfers between devices  215 us (27%)
  other arithmetic  207 us (26%)
  local copies, waits for them, and re-layouts  157 us (20%)
  matrix products  128 us (16%)
  starting transfers between devices  63.6 us (8%)
    ppermute x45, waiting for transfers between devices, swapped(): lax.ppermute(x, axis, [(i, i ^ bit) for i in range(lax.axis_size(axis))])  208 us
    dot_general x19, matrix products, mm(): jnp.einsum(spec, a.astype(low), b.astype(low), preferred_element_type=wide)  89.4 us
    ppermute x45, starting transfers between devices, swapped(): lax.ppermute(x, axis, [(i, i ^ bit) for i in range(lax.axis_size(axis))])  40 us
    unnamed x353, local copies, waits for them, and re-layouts  39.7 us
    ppermute x12, starting transfers between devices, shifted(): return lax.ppermute(x, axis, pairs)  23.6 us
    add x8, other arithmetic, owner_stages(): held = (yield (keep + swapped(send, 'fsdp', bit).astype(wide)))  22 us
    dynamic_slice x6, local copies, waits for them, and re-layouts, owner_stages(): keep = lax.dynamic_index_in_dim(pair, side, 1, False)  21.4 us
    mul x1, other arithmetic, body(): xc = pre * jax.nn.sigmoid(pre)  21.1 us
  transfers between devices with their start and end apart: 57, of which 27 were waited for; matrix products, arithmetic and copies ran while one was open for 38% of the time, Pallas kernels for 0%

profile of v2, /device:TPU:0, one launch (start us, length us, event | category | flops | bytes accessed | tf_op | source)
XLA Modules:
  0.0 775.9 jit_solution(16063210664150475964)
XLA Ops:
  2.8 4.1 concatenate.75
  20.9 20.7 %collective-permute-done.2 = bf16[1,256,2304]{2,1,0:T(8,128)(2,1)} collective-permute-done((bf16[1,256,2304]{2,1,0:T(8,128)(2,1)S(1)}, bf16[1,256,2304]{2,1,0:T(8,128)(2,1)}, u32[]{:S(2)}, u32[]{:S(2)}) %collective-permute-start.2) | collective-permute-done | bytes 1179680 | tf_op jit(solution)/shard_map/ppermute | solution.py:31
  56.8 5.1 fusion.123
  62.0 3.6 copy-done.2
  66.2 3.4 collective-permute-start.4
  73.2 21.1 %fusion.10 = (f32[1024,2304]{1,0:T(8,128)S(1)}, f32[1024,2304]{1,0:T(8,128)}) fusion(f32[1024]{0:T(1024)S(1)} %get-tuple-element.240, f32[1024,2304]{1,0:T(8,128)} %copy-done.2, f32[2304]{0:T(1024)} %get-tuple-element.106, f32[1024]{0:T(1024)} %get-tuple-element.239, f32[2304]{0:T(1024)} %get-tuple-element.107, f32[3,2304]{1,0:T(4,128)} %collective-permute-done.4, ...), kind=kLoop, calls=%fused_computation.26 | loop fusion | flops 44826624 | bytes 28401664 | tf_op jit(solution)/shard_map/mul | solution.py:200
  95.2 4.4 slice.364
  99.6 9.1 %copy.71 = f32[8,128,2048]{1,2,0:T(8,128)} copy(f32[8,128,2048]{2,1,0:T(8,128)} %bitcast.428) | data formatting | bytes 16777216 | tf_op jit(solution)/shard_map/reshape | solution.py:228
  108.8 5.0 multiply_convert_fusion.5
  117.9 5.4 add_convert_fusion.1
  135.7 3.9 collective-permute-start.9
  142.2 6.1 collective-permute-done.9
  160.4 36.8 %collective-permute-done.10 = bf16[1,256,2048]{2,1,0:T(8,128)(2,1)S(1)} collective-permute-done((bf16[1,256,2048]{2,1,0:T(8,128)(2,1)}, bf16[1,256,2048]{2,1,0:T(8,128)(2,1)S(1)}, u32[]{:S(2)}, u32[]{:S(2)}) %collective-permute-start.10) | collective-permute-done | bytes 1048608 | tf_op jit(solution)/shard_map/ppermute | solution.py:31
  201.0 3.6 slice-done.1
  204.7 9.6 %multiply_add_fusion.2 = f32[8,32,64,128]{3,2,1,0:T(8,128)} fusion(f32[8,32,64,128]{3,2,1,0:T(8,128)S(1)} %bitcast.414, f32[8,32,64,128]{3,2,1,0:T(8,128)S(1)} %bitcast.426, f32[32]{0:T(128)S(1)} %copy-done.144, f32[8,32,128]{2,1,0:T(8,128)S(1)} %copy-done.86, f32[8,128,128]{2,1,0:T(8,128)S(1)} %fusion.145, f32[8,32,128]{2,1,0:T(8,128)S(1)} %copy-done.80, ...), kind=kOutput, calls=%fused_computation.50 | convolution fusion | flops 566231040 | bytes 26099840 | tf_op jit(solution)/shard_map/chps,chts->chpt/dot_general | solution.py:35
  214.3 9.1 %copy.73 = f32[8,128,2048]{2,1,0:T(8,128)} copy(f32[8,128,2048]{1,2,0:T(8,128)} %bitcast.461) | data formatting | bytes 16777216 | tf_op jit(solution)/shard_map/transpose | solution.py:231
  233.0 10.8 %multiply_reduce_fusion.12 = (f32[1024]{0:T(1024)S(1)}, f32[1024,2048]{1,0:T(8,128)S(1)}, f32[1024,2048]{1,0:T(8,128)}) fusion(f32[8,128,2048]{2,1,0:T(8,128)S(1)} %bitcast.431, bf16[1024,2048]{1,0:T(8,128)(2,1)} %bitcast.474, bf16[1024,1024]{1,0:T(8,128)(2,1)S(1)} %copy-done.9, f32[1024]{0:T(1024)S(1)} %bitcast.516, f32[1024]{0:T(1024)S(1)} %copy-done.100), kind=kOutput, calls=%fused_computation.47 | convolution fusion | flops 4313840640 | bytes 31469568 | tf_op jit(solution)/shard_map/dot_general | solution.py:277
  243.8 3.7 select_bitcast_fusion.3
  249.6 7.3 fusion.114
  256.9 8.1 %fusion.13 = (f32[2048]{0:T(1024)S(1)}, f32[1024]{0:T(1024)S(1)}, f32[2048,1024]{0,1:T(8,128)}) fusion(f32[1024,2048]{1,0:T(8,128)S(1)} %get-tuple-element.140, f32[1024]{0:T(1024)S(1)} %add_rsqrt_fusion, f32[2048]{0:T(1024)S(1)} %bitcast.524, bf16[2048,1024]{1,0:T(8,128)(2,1)S(1)} %bitcast.476, bf16[1024,1024]{1,0:T(8,128)(2,1)S(1)} %copy-done.64), kind=kOutput, calls=%fused_computation.32 | convolution fusion | flops 4307547136 | bytes 23093248 | tf_op jit(solution)/shard_map/dot_general | solution.py:285
  265.0 3.8 fusion.44
  269.3 14.7 %fusion.15 = (bf16[1024,2048]{1,0:T(8,128)(2,1)}, f32[1024,2048]{1,0:T(8,128)}) fusion(f32[8,128,2048]{2,1,0:T(8,128)S(1)} %bitcast.431, f32[1024,2048]{1,0:T(8,128)} %get-tuple-element.260, f32[1024]{0:T(1024)S(1)} %broadcast_multiply_fusion, f32[1024,2048]{1,0:T(8,128)S(1)} %get-tuple-element.140, f32[2048,1024]{0,1:T(8,128)} %get-tuple-element.261, ...), kind=kLoop, calls=%fused_computation.36 | loop fusion | flops 35651584 | bytes 46153728 | tf_op jit(solution)/shard_map/convert_element_type | solution.py:291
  284.0 6.7 fusion.118
  295.7 3.9 copy.101
  299.7 10.0 %fusion.148 = f32[1024,1024]{1,0:T(8,128)} fusion(bf16[1024,2048]{1,0:T(8,128)(2,1)} %get-tuple-element.153, bf16[1024,2048]{1,0:T(8,128)(2,1)} %bitcast.475), kind=kOutput, calls=%fused_computation.397 | convolution fusion | flops 4294967296 | bytes 12582912 | tf_op jit(solution)/shard_map/te,de->td/dot_general | solution.py:35
  310.2 4.7 constant_dynamic-slice_fusion.8
  314.9 5.7 copy.79
  320.7 10.4 %fusion.38 = bf16[1024,1024]{1,0:T(8,128)(2,1)} fusion(bf16[1024,1024]{1,0:T(8,128)(2,1)S(1)} %copy-done.9, bf16[2048,1024]{1,0:T(8,128)(2,1)} %bitcast.477, f32[1024,2048]{1,0:T(8,128)} %copy-done.48, f32[2048]{0:T(1024)S(1)} %bitcast.526, f32[1024]{0:T(1024)S(1)} %add_rsqrt_fusion), kind=kOutput, calls=%fused_computation.80 | convolution fusion | flops 4304404480 | bytes 16789504 | tf_op jit(solution)/shard_map/dot_general | solution.py:283
  331.1 5.9 bitcast_add_fusion.1
  337.0 9.1 %copy.78 = f32[8,128,2048]{1,2,0:T(8,128)} copy(f32[8,128,2048]{2,1,0:T(8,128)} %bitcast.433) | data formatting | bytes 16777216 | tf_op jit(solution)/shard_map/reshape | solution.py:228
  346.2 5.6 bitcast_add_fusion
  352.9 10.7 %multiply_reduce_fusion.6 = (f32[32]{0:T(128)S(1)}, f32[8,32,128]{2,1,0:T(8,128)S(1)}, bf16[8,32,64,128]{3,2,1,0:T(8,128)(2,1)S(1)}, bf16[8,32,64,128]{3,2,1,0:T(8,128)(2,1)}) fusion(f32[8,32,64,128]{3,2,1,0:T(8,128)} %bitcast.411, f32[8,32,64,128]{3,2,1,0:T(8,128)S(1)} %bitcast.419, f32[8,32,128]{2,1,0:T(8,128)S(1)} %copy-done.86, f32[8,2048,128]{2,1,0:T(8,128)} %copy-done.6), kind=kLoop, calls=%fused_computation.37 | loop fusion | flops 16744416 | bytes 33816704 | tf_op jit(solution)/shard_map/reduce_sum | solution.py:298
  367.7 5.1 add_convert_fusion
  379.6 4.1 collective-permute-start.16
  387.1 5.7 fusion.147
  400.9 4.4 multiply_reduce_fusion.7
  412.7 12.2 %collective-permute-done.16 = bf16[1,512,1024]{2,1,0:T(8,128)(2,1)} collective-permute-done((bf16[1,512,1024]{2,1,0:T(8,128)(2,1)}, bf16[1,512,1024]{2,1,0:T(8,128)(2,1)}, u32[]{:S(2)}, u32[]{:S(2)}) %collective-permute-start.16) | collective-permute-done | bytes 1048608 | tf_op jit(solution)/shard_map/ppermute | solution.py:31
  426.5 14.3 %multiply_reduce_fusion = (f32[8,32,128]{2,1,0:T(8,128)S(1)}, f32[8,32,128]{2,1,0:T(8,128)S(1)}, bf16[8,128,128]{2,1,0:T(8,128)(2,1)S(1)}) fusion(f32[8,128,128]{2,1,0:T(8,128)S(1)} %copy-done.88, f32[8,32,128]{2,1,0:T(8,128)S(1)} %copy-done.81, pred[128,128]{1,0:T(8,128)(4,1)S(1)} %copy-done.108, bf16[8,32,64,128]{3,2,1,0:T(8,128)(2,1)S(1)} %copy-done.58, ...), kind=kOutput, calls=%fused_computation.3 | convolution fusion | flops 570228736 | bytes 13910016 | tf_op jit(solution)/shard_map/chpt,chps->chts/dot_general | solution.py:35
  444.1 9.9 %multiply_add_fusion.3 = f32[8,32,64,128]{3,2,1,0:T(8,128)} fusion(f32[8,32,64,128]{3,2,1,0:T(8,128)S(1)} %bitcast.429, f32[8,32,128]{2,1,0:T(8,128)S(1)} %copy-done.74, bf16[8,32,64,128]{3,2,1,0:T(8,128)(2,1)S(1)} %copy-done.58, f32[8,128,128]{2,1,0:T(8,128)S(1)} %copy-done.88, f32[8,32,128]{2,1,0:T(8,128)S(1)} %copy-done.81, ...), kind=kOutput, calls=%fused_computation.62 | convolution fusion | flops 557842432 | bytes 21774336 | tf_op jit(solution)/shard_map/chts,chpt->chps/dot_general | solution.py:35
  459.1 16.0 %collective-permute-done.24 = bf16[128,1024]{1,0:T(8,128)(2,1)S(1)} collective-permute-done((bf16[128,1024]{1,0:T(8,128)(2,1)S(1)}, bf16[128,1024]{1,0:T(8,128)(2,1)S(1)}, u32[]{:S(2)}, u32[]{:S(2)}) %collective-permute-start.24) | collective-permute-done | bytes 262176 | tf_op jit(solution)/shard_map/ppermute | solution.py:31
  477.1 13.5 %multiply_reduce_fusion.8 = (f32[8,32,128]{2,1,0:T(8,128)S(1)}, f32[8,32,128]{2,1,0:T(8,128)S(1)}, f32[8,32,64,128]{3,2,1,0:T(8,128)}) fusion(f32[8,2048,128]{2,1,0:T(8,128)} %copy-done.7, f32[8,32,128]{2,1,0:T(8,128)S(1)} %copy-done.74, f32[8,32,128]{2,1,0:T(8,128)S(1)} %copy-done.76, f32[8,128,2048]{1,2,0:T(8,128)S(1)} %bitcast.416, ...), kind=kLoop, calls=%fused_computation.39 | loop fusion | flops 18808832 | bytes 42467456 | tf_op jit(solution)/shard_map/reduce_sum | solution.py:319
  502.3 9.1 %copy.81 = f32[8,128,2048]{2,1,0:T(8,128)} copy(f32[8,128,2048]{1,2,0:T(8,128)} %bitcast.432) | data formatting | bytes 16777216 | tf_op jit(solution)/shard_map/transpose | solution.py:231
  511.5 6.0 collective-permute-done.26
  517.5 11.2 %collective-permute-done.27 = bf16[64,2048]{0,1:T(8,128)(2,1)S(1)} collective-permute-done((bf16[64,2048]{0,1:T(8,128)(2,1)S(1)}, bf16[64,2048]{0,1:T(8,128)(2,1)S(1)}, u32[]{:S(2)}, u32[]{:S(2)}) %collective-permute-start.27) | collective-permute-done | bytes 262176 | tf_op jit(solution)/shard_map/ppermute | solution.py:31
  530.0 8.8 %maximum_multiply_fusion = f32[1024,2304]{1,0:T(8,128)S(1)} fusion(f32[1024,128]{1,0:T(8,128)S(1)} %bitcast.490, f32[1024,128]{1,0:T(8,128)S(1)} %bitcast.491, f32[1024,2048]{1,0:T(8,128)} %bitcast.427, f32[1024,2304]{1,0:T(8,128)} %get-tuple-element.152), kind=kLoop, calls=%fused_computation.20 | loop fusion | flops 23592960 | bytes 28311552 | tf_op jit(solution)/shard_map/mul | solution.py:338
  539.7 3.7 collective-permute-done.29
  544.3 4.2 constant_dynamic-update-slice_fusion.1
  548.6 10.1 %multiply_reduce_fusion.5 = (f32[2304]{0:T(1024)S(1)}, f32[2304]{0:T(1024)S(1)}, f32[2304]{0:T(1024)S(1)}, f32[2304]{0:T(1024)S(1)}, f32[2304]{0:T(1024)}) fusion(f32[1024,2304]{1,0:T(8,128)S(1)} %maximum_multiply_fusion, f32[1024]{0:T(1024)} %get-tuple-element.243, f32[1024,2304]{1,0:T(8,128)S(1)} %bitcast.421, f32[3,2304]{1,0:T(4,128)} %collective-permute-done.4, ...), kind=kLoop, calls=%fused_computation.24 | loop fusion | flops 37737216 | bytes 18964480 | tf_op jit(solution)/shard_map/reduce_sum | solution.py:344
  561.5 3.8 collective-permute-start.31
  568.3 17.3 %fusion.6 = bf16[1024,2304]{1,0:T(8,128)(2,1)S(1)} fusion(f32[1027,2304]{1,0:T(8,128)} %constant_dynamic-update-slice_fusion, f32[1024,2304]{1,0:T(8,128)} %copy-done, f32[1024]{0:T(1024)} %get-tuple-element.241, f32[1024]{0:T(1024)} %get-tuple-element.242, f32[1024]{0:T(1024)} %get-tuple-element.237, f32[1024]{0:T(1024)} %copy-done.97, ...), kind=kLoop, calls=%fused_computation.13 | loop fusion | flops 28311552 | bytes 42520576 | tf_op jit(solution)/shard_map/convert_element_type | solution.py:355
  595.1 4.8 fusion.42
  606.4 20.2 %collective-permute-done.40 = bf16[64,2048]{0,1:T(8,128)(2,1)} collective-permute-done((bf16[64,2048]{0,1:T(8,128)(2,1)}, bf16[64,2048]{0,1:T(8,128)(2,1)}, u32[]{:S(2)}, u32[]{:S(2)}) %collective-permute-start.40) | collective-permute-done | bytes 262176 | tf_op jit(solution)/shard_map/ppermute | solution.py:31
  649.7 5.1 fusion.149
  654.9 3.5 fusion.36
  682.1 5.5 collective-permute-done.49
  689.5 7.5 collective-permute-done.42
  699.7 5.4 collective-permute-done.43
  706.5 5.7 collective-permute-done.51
  715.6 4.1 collective-permute-done.52
  721.7 6.8 collective-permute-done.45
  732.0 19.0 %collective-permute-done.46 = bf16[32,1152]{0,1:T(8,128)(2,1)S(1)} collective-permute-done((bf16[32,1152]{0,1:T(8,128)(2,1)S(1)}, bf16[32,1152]{0,1:T(8,128)(2,1)S(1)}, u32[]{:S(2)}, u32[]{:S(2)}) %collective-permute-start.46) | collective-permute-done | bytes 73760 | tf_op jit(solution)/shard_map/ppermute | solution.py:31
  751.3 6.0 collective-permute-done.54
  757.8 5.8 collective-permute-done.47
  764.1 5.7 collective-permute-done.55
  (647 shorter events, 234.9 us)
Async XLA Ops:
  7.0 8.9 %collective-permute-start = (bf16[1,1,11864]{2,1,0:T(2,128)(2,1)S(1)}, bf16[1,1,11864]{2,1,0:T(2,128)(2,1)S(1)}, u32[]{:S(2)}, u32[]{:S(2)}) collective-permute-start(bf16[1,1,11864]{2,1,0:T(2,128)(2,1)S(1)} %broadcast_in_dim_broadcast_in_dim.3), channel_id=1, source_target_pairs={{0,2},{1,3},{2,0},{3,1},{4,6},{5,7},{6,4},{7,5},{8,10},{9,11},{10,... | collective-permute-start | bytes 71192 | tf_op jit(solution)/shard_map/ppermute | solution.py:31
  14.0 27.6 %collective-permute-start.2 = (bf16[1,256,2304]{2,1,0:T(8,128)(2,1)S(1)}, bf16[1,256,2304]{2,1,0:T(8,128)(2,1)}, u32[]{:S(2)}, u32[]{:S(2)}) collective-permute-start(bf16[1,256,2304]{2,1,0:T(8,128)(2,1)S(1)} %bitcast.462), channel_id=1, source_target_pairs={{0,2},{1,3},{2,0},{3,1},{4,6},{5,7},{6,4},{7,5},{8,10},{9,11},{10,... | collective-permute-start | bytes 3538952 | tf_op jit(solution)/shard_map/ppermute | solution.py:31
  15.9 57.3 %copy-start.97 = (f32[1024]{0:T(1024)}, f32[1024]{0:T(1024)S(1)}, u32[]{:S(2)}) copy-start(f32[1024]{0:T(1024)S(1)} %get-tuple-element.240) | copy-start | bytes 12292
  15.9 40.7 %copy-start.99 = (f32[1024]{0:T(1024)}, f32[1024]{0:T(1024)S(1)}, u32[]{:S(2)}) copy-start(f32[1024]{0:T(1024)S(1)} %add_rsqrt_fusion.1) | copy-start | bytes 12292
  16.1 4.6 collective-permute-start.1
  45.6 7.8 %collective-permute-start.3 = (bf16[2,256,2304]{2,1,0:T(8,128)(2,1)}, bf16[2,256,2304]{2,1,0:T(8,128)(2,1)}, u32[]{:S(2)}, u32[]{:S(2)}) collective-permute-start(bf16[2,256,2304]{2,1,0:T(8,128)(2,1)} %maximum_bitcast_fusion), channel_id=1, source_target_pairs={{0,1},{1,0},{2,3},{3,2},{4,5},{5,4},{6,7},{7,6},{8,9},{9,8},{10,11... | collective-permute-start | bytes 7077896 | tf_op jit(solution)/shard_map/ppermute | solution.py:31
  51.8 148.5 %copy-start.75 = (f32[8,32,128]{2,1,0:T(8,128)}, f32[8,32,128]{2,1,0:T(8,128)S(1)}, u32[]{:S(2)}) copy-start(f32[8,32,128]{2,1,0:T(8,128)S(1)} %bitcast_bitcast_fusion) | copy-start | bytes 393220
  53.5 55.3 %copy-start.73 = (f32[8,32,128]{2,1,0:T(8,128)}, f32[8,32,128]{2,1,0:T(8,128)S(1)}, u32[]{:S(2)}) copy-start(f32[8,32,128]{2,1,0:T(8,128)S(1)} %get-tuple-element.227) | copy-start | bytes 393220
  66.2 7.1 collective-permute-start.4
  123.4 30.2 %collective-permute-start.8 = (bf16[32,64,128]{2,1,0:T(8,128)(2,1)}, bf16[32,64,128]{2,1,0:T(8,128)(2,1)}, u32[]{:S(2)}, u32[]{:S(2)}) collective-permute-start(bf16[32,64,128]{2,1,0:T(8,128)(2,1)} %get-tuple-element.147), channel_id=1, source_target_pairs={{0,3},{4,7},{8,11},{12,15},{16,19},{20,23},{24,27},{28,31}} | collective-permute-start | bytes 1572872 | tf_op jit(solution)/shard_map/ppermute | solution.py:23
  125.5 28.1 %collective-permute-start.6 = (bf16[32,64,128]{2,1,0:T(8,128)(2,1)}, bf16[32,64,128]{2,1,0:T(8,128)(2,1)}, u32[]{:S(2)}, u32[]{:S(2)}) collective-permute-start(bf16[32,64,128]{2,1,0:T(8,128)(2,1)} %get-tuple-element.147), channel_id=1, source_target_pairs={{0,2},{1,3},{4,6},{5,7},{8,10},{9,11},{12,14},{13,15},{16,18},{17,... | collective-permute-start | bytes 1572872 | tf_op jit(solution)/shard_map/ppermute | solution.py:23
  127.6 26.0 %collective-permute-start.5 = (bf16[32,64,128]{2,1,0:T(8,128)(2,1)}, bf16[32,64,128]{2,1,0:T(8,128)(2,1)}, u32[]{:S(2)}, u32[]{:S(2)}) collective-permute-start(bf16[32,64,128]{2,1,0:T(8,128)(2,1)} %get-tuple-element.147), channel_id=1, source_target_pairs={{0,1},{1,2},{2,3},{4,5},{5,6},{6,7},{8,9},{9,10},{10,11},{12,13},{... | collective-permute-start | bytes 1572872 | tf_op jit(solution)/shard_map/ppermute | solution.py:23
  130.3 5.4 collective-permute-start.21
  131.6 8.0 %collective-permute-start.19 = (f32[32]{0:T(128)S(1)}, f32[32]{0:T(128)S(1)}, u32[]{:S(2)}, u32[]{:S(2)}) collective-permute-start(f32[32]{0:T(128)S(1)} %exp.47), channel_id=1, source_target_pairs={{1,0},{2,1},{3,2},{5,4},{6,5},{7,6},{9,8},{10,9},{11,10},{13,12},{... | collective-permute-start | bytes 392 | tf_op jit(solution)/shard_map/ppermute | solution.py:23
  135.7 12.6 %collective-permute-start.9 = (f32[32]{0:T(128)S(1)}, f32[32]{0:T(128)S(1)}, u32[]{:S(2)}, u32[]{:S(2)}) collective-permute-start(f32[32]{0:T(128)S(1)} %exp.47), channel_id=1, source_target_pairs={{0,2},{1,3},{4,6},{5,7},{8,10},{9,11},{12,14},{13,15},{16,18},{17,... | collective-permute-start | bytes 392 | tf_op jit(solution)/shard_map/ppermute | solution.py:23
  139.6 8.7 %collective-permute-start.7 = (f32[32]{0:T(128)S(1)}, f32[32]{0:T(128)S(1)}, u32[]{:S(2)}, u32[]{:S(2)}) collective-permute-start(f32[32]{0:T(128)S(1)} %exp.47), channel_id=1, source_target_pairs={{0,1},{1,2},{2,3},{4,5},{5,6},{6,7},{8,9},{9,10},{10,11},{12,13},{... | collective-permute-start | bytes 392 | tf_op jit(solution)/shard_map/ppermute | solution.py:23
  148.3 75.2 %collective-permute-start.12 = (bf16[1,512,1024]{2,1,0:T(8,128)(2,1)}, bf16[1,512,1024]{2,1,0:T(8,128)(2,1)}, u32[]{:S(2)}, u32[]{:S(2)}) collective-permute-start(bf16[1,512,1024]{2,1,0:T(8,128)(2,1)} %bitcast.512), channel_id=1, source_target_pairs={{0,2},{1,3},{2,0},{3,1},{4,6},{5,7},{6,4},{7,5},{8,10},{9,11},{10,... | collective-permute-start | bytes 3145736 | tf_op jit(solution)/shard_map/ppermute | solution.py:31
  151.0 46.1 %collective-permute-start.10 = (bf16[1,256,2048]{2,1,0:T(8,128)(2,1)}, bf16[1,256,2048]{2,1,0:T(8,128)(2,1)S(1)}, u32[]{:S(2)}, u32[]{:S(2)}) collective-permute-start(bf16[1,256,2048]{2,1,0:T(8,128)(2,1)} %bitcast.473), channel_id=1, source_target_pairs={{0,2},{1,3},{2,0},{3,1},{4,6},{5,7},{6,4},{7,5},{8,10},{9,11},{10,... | collective-permute-start | bytes 3145736 | tf_op jit(solution)/shard_map/ppermute | solution.py:31
  153.6 46.8 %copy-start.87 = (f32[8,128,128]{2,1,0:T(8,128)}, f32[8,128,128]{2,1,0:T(8,128)S(1)}, u32[]{:S(2)}) copy-start(f32[8,128,128]{2,1,0:T(8,128)S(1)} %fusion.145) | copy-start | bytes 1572868
  160.3 38.7 %copy-start.8 = (bf16[8,2048,128]{2,1,0:T(8,128)(2,1)}, bf16[8,2048,128]{2,1,0:T(8,128)(2,1)S(1)}, u32[]{:S(2)}) copy-start(bf16[8,2048,128]{2,1,0:T(8,128)(2,1)S(1)} %bitcast_dynamic-update-slice_fusion.24) | copy-start | bytes 12582916
  160.3 38.7 %copy-start.20 = (f32[1024,128]{1,0:T(8,128)S(1)}, f32[1024,128]{1,0:T(8,128)}, u32[]{:S(2)}) copy-start(f32[1024,128]{1,0:T(8,128)} %get-tuple-element.155) | copy-start | bytes 1572868
  198.9 27.9 %collective-permute-start.11 = (bf16[2,256,2048]{2,1,0:T(8,128)(2,1)}, bf16[2,256,2048]{2,1,0:T(8,128)(2,1)}, u32[]{:S(2)}, u32[]{:S(2)}) collective-permute-start(bf16[2,256,2048]{2,1,0:T(8,128)(2,1)} %maximum_bitcast_fusion.1), channel_id=1, source_target_pairs={{0,1},{1,0},{2,3},{3,2},{4,5},{5,4},{6,7},{7,6},{8,9},{9,8},{10,11... | collective-permute-start | bytes 6291464 | tf_op jit(solution)/shard_map/ppermute | solution.py:31
  226.8 17.0 %collective-permute-start.13 = (bf16[2,512,1024]{2,1,0:T(8,128)(2,1)}, bf16[2,512,1024]{2,1,0:T(8,128)(2,1)}, u32[]{:S(2)}, u32[]{:S(2)}) collective-permute-start(bf16[2,512,1024]{2,1,0:T(8,128)(2,1)} %maximum_bitcast_fusion.2), channel_id=1, source_target_pairs={{0,1},{1,0},{2,3},{3,2},{4,5},{5,4},{6,7},{7,6},{8,9},{9,8},{10,11... | collective-permute-start | bytes 6291464 | tf_op jit(solution)/shard_map/ppermute | solution.py:31
  268.8 62.3 %collective-permute-start.14 = (bf16[2,512,1024]{2,1,0:T(8,128)(2,1)}, bf16[2,512,1024]{2,1,0:T(8,128)(2,1)}, u32[]{:S(2)}, u32[]{:S(2)}) collective-permute-start(bf16[2,512,1024]{2,1,0:T(8,128)(2,1)} %fusion.44), channel_id=1, source_target_pairs={{0,1},{1,0},{2,3},{3,2},{4,5},{5,4},{6,7},{7,6},{8,9},{9,8},{10,11... | collective-permute-start | bytes 6291464 | tf_op jit(solution)/shard_map/ppermute | solution.py:31
  299.6 46.5 %collective-permute-start.15 = (bf16[2,256,2048]{1,2,0:T(8,128)(2,1)}, bf16[2,256,2048]{1,2,0:T(8,128)(2,1)}, u32[]{:S(2)}, u32[]{:S(2)}) collective-permute-start(bf16[2,256,2048]{1,2,0:T(8,128)(2,1)} %bitcast.508), channel_id=1, source_target_pairs={{0,1},{1,0},{2,3},{3,2},{4,5},{5,4},{6,7},{7,6},{8,9},{9,8},{10,11... | collective-permute-start | bytes 6291464 | tf_op jit(solution)/shard_map/ppermute | solution.py:31
  372.8 20.0 %collective-permute-start.20 = (bf16[32,64,128]{2,1,0:T(8,128)(2,1)}, bf16[32,64,128]{2,1,0:T(8,128)(2,1)}, u32[]{:S(2)}, u32[]{:S(2)}) collective-permute-start(bf16[32,64,128]{2,1,0:T(8,128)(2,1)} %get-tuple-element.135), channel_id=1, source_target_pairs={{3,0},{7,4},{11,8},{15,12},{19,16},{23,20},{27,24},{31,28}} | collective-permute-start | bytes 1572872 | tf_op jit(solution)/shard_map/ppermute | solution.py:23
  374.1 18.7 %collective-permute-start.18 = (bf16[32,64,128]{2,1,0:T(8,128)(2,1)}, bf16[32,64,128]{2,1,0:T(8,128)(2,1)}, u32[]{:S(2)}, u32[]{:S(2)}) collective-permute-start(bf16[32,64,128]{2,1,0:T(8,128)(2,1)} %get-tuple-element.135), channel_id=1, source_target_pairs={{2,0},{3,1},{6,4},{7,5},{10,8},{11,9},{14,12},{15,13},{18,16},{19,... | collective-permute-start | bytes 1572872 | tf_op jit(solution)/shard_map/ppermute | solution.py:23
  375.4 17.4 %collective-permute-start.17 = (bf16[32,64,128]{2,1,0:T(8,128)(2,1)}, bf16[32,64,128]{2,1,0:T(8,128)(2,1)}, u32[]{:S(2)}, u32[]{:S(2)}) collective-permute-start(bf16[32,64,128]{2,1,0:T(8,128)(2,1)} %get-tuple-element.135), channel_id=1, source_target_pairs={{1,0},{2,1},{3,2},{5,4},{6,5},{7,6},{9,8},{10,9},{11,10},{13,12},{... | collective-permute-start | bytes 1572872 | tf_op jit(solution)/shard_map/ppermute | solution.py:23
  379.6 45.2 %collective-permute-start.16 = (bf16[1,512,1024]{2,1,0:T(8,128)(2,1)}, bf16[1,512,1024]{2,1,0:T(8,128)(2,1)}, u32[]{:S(2)}, u32[]{:S(2)}) collective-permute-start(bf16[1,512,1024]{2,1,0:T(8,128)(2,1)} %dynamic-slice_convert_fusion.1), channel_id=1, source_target_pairs={{0,2},{1,3},{2,0},{3,1},{4,6},{5,7},{6,4},{7,5},{8,10},{9,11},{10,... | collective-permute-start | bytes 3145736 | tf_op jit(solution)/shard_map/ppermute | solution.py:31
  387.0 67.0 %collective-permute-start.23 = (bf16[1,256,2048]{1,2,0:T(8,128)(2,1)}, bf16[1,256,2048]{1,2,0:T(8,128)(2,1)}, u32[]{:S(2)}, u32[]{:S(2)}) collective-permute-start(bf16[1,256,2048]{1,2,0:T(8,128)(2,1)} %dynamic-slice_convert_fusion), channel_id=1, source_target_pairs={{0,2},{1,3},{2,0},{3,1},{4,6},{5,7},{6,4},{7,5},{8,10},{9,11},{10,... | collective-permute-start | bytes 3145736 | tf_op jit(solution)/shard_map/ppermute | solution.py:31
  440.9 14.6 %collective-permute-start.22 = (bf16[256,1024]{1,0:T(8,128)(2,1)S(1)}, bf16[256,1024]{1,0:T(8,128)(2,1)S(1)}, u32[]{:S(2)}, u32[]{:S(2)}) collective-permute-start(bf16[256,1024]{1,0:T(8,128)(2,1)S(1)} %fusion.46), channel_id=1, source_target_pairs={{0,4},{4,0},{8,12},{12,8},{16,20},{20,16},{24,28},{28,24},{1,5},{5... | collective-permute-start | bytes 1572872 | tf_op jit(solution)/shard_map/ppermute | solution.py:31
  455.8 20.2 %collective-permute-start.25 = (bf16[128,2048]{0,1:T(8,128)(2,1)S(1)}, bf16[128,2048]{0,1:T(8,128)(2,1)S(1)}, u32[]{:S(2)}, u32[]{:S(2)}) collective-permute-start(bf16[128,2048]{0,1:T(8,128)(2,1)S(1)} %fusion.47), channel_id=1, source_target_pairs={{0,8},{4,12},{8,0},{12,4},{16,24},{20,28},{24,16},{28,20},{1,9},{5... | collective-permute-start | bytes 1572872 | tf_op jit(solution)/shard_map/ppermute | solution.py:31
  457.4 17.6 %collective-permute-start.24 = (bf16[128,1024]{1,0:T(8,128)(2,1)S(1)}, bf16[128,1024]{1,0:T(8,128)(2,1)S(1)}, u32[]{:S(2)}, u32[]{:S(2)}) collective-permute-start(bf16[128,1024]{1,0:T(8,128)(2,1)S(1)} %dynamic-slice_convert_fusion.14), channel_id=1, source_target_pairs={{0,8},{4,12},{8,0},{12,4},{16,24},{20,28},{24,16},{28,20},{1,9},{5... | collective-permute-start | bytes 786440 | tf_op jit(solution)/shard_map/ppermute | solution.py:31
  496.1 21.4 %collective-permute-start.26 = (bf16[64,1024]{1,0:T(8,128)(2,1)S(1)}, bf16[64,1024]{1,0:T(8,128)(2,1)S(1)}, u32[]{:S(2)}, u32[]{:S(2)}) collective-permute-start(bf16[64,1024]{1,0:T(8,128)(2,1)S(1)} %dynamic-slice_convert_fusion.15), channel_id=1, source_target_pairs={{0,16},{4,20},{8,24},{12,28},{16,0},{20,4},{24,8},{28,12},{1,17},{... | collective-permute-start | bytes 393224 | tf_op jit(solution)/shard_map/ppermute | solution.py:31
  499.0 29.7 %collective-permute-start.27 = (bf16[64,2048]{0,1:T(8,128)(2,1)S(1)}, bf16[64,2048]{0,1:T(8,128)(2,1)S(1)}, u32[]{:S(2)}, u32[]{:S(2)}) collective-permute-start(bf16[64,2048]{0,1:T(8,128)(2,1)S(1)} %dynamic-slice_convert_fusion.5), channel_id=1, source_target_pairs={{0,16},{4,20},{8,24},{12,28},{16,0},{20,4},{24,8},{28,12},{1,17},{... | collective-permute-start | bytes 786440 | tf_op jit(solution)/shard_map/ppermute | solution.py:31
  529.0 9.8 %collective-permute-start.28 = (bf16[64,1024]{1,0:T(8,128)(2,1)S(1)}, bf16[64,1024]{1,0:T(8,128)(2,1)S(1)}, u32[]{:S(2)}, u32[]{:S(2)}) collective-permute-start(bf16[64,1024]{1,0:T(8,128)(2,1)S(1)} %convert_add_fusion.10), channel_id=1, source_target_pairs={{0,16},{4,20},{8,24},{12,28},{16,0},{20,4},{24,8},{28,12},{1,17},{... | collective-permute-start | bytes 393224 | tf_op jit(solution)/shard_map/ppermute | solution.py:31
  529.3 14.0 %collective-permute-start.29 = (bf16[32,2048]{0,1:T(8,128)(2,1)S(1)}, bf16[32,2048]{0,1:T(8,128)(2,1)S(1)}, u32[]{:S(2)}, u32[]{:S(2)}) collective-permute-start(bf16[32,2048]{0,1:T(8,128)(2,1)S(1)} %dynamic-slice_convert_fusion.4), channel_id=1, source_target_pairs={{0,4},{4,0},{8,12},{12,8},{16,20},{20,16},{24,28},{28,24},{1,5},{5... | collective-permute-start | bytes 393224 | tf_op jit(solution)/shard_map/ppermute | solution.py:31
  560.2 7.5 collective-permute-start.30
  561.5 27.0 %collective-permute-start.31 = (bf16[128,1024]{1,0:T(8,128)(2,1)}, bf16[128,1024]{1,0:T(8,128)(2,1)}, u32[]{:S(2)}, u32[]{:S(2)}) collective-permute-start(bf16[128,1024]{1,0:T(8,128)(2,1)} %pad_maximum_fusion.12), channel_id=1, source_target_pairs={{0,8},{4,12},{8,0},{12,4},{16,24},{20,28},{24,16},{28,20},{1,9},{5... | collective-permute-start | bytes 786440 | tf_op jit(solution)/shard_map/ppermute | solution.py:31
  565.3 20.4 %collective-permute-start.32 = (bf16[32,2048]{0,1:T(8,128)(2,1)S(1)}, bf16[32,2048]{0,1:T(8,128)(2,1)}, u32[]{:S(2)}, u32[]{:S(2)}) collective-permute-start(bf16[32,2048]{0,1:T(8,128)(2,1)S(1)} %convert_add_fusion.5), channel_id=1, source_target_pairs={{0,4},{4,0},{8,12},{12,8},{16,20},{20,16},{24,28},{28,24},{1,5},{5... | collective-permute-start | bytes 393224 | tf_op jit(solution)/shard_map/ppermute | solution.py:31
  599.9 26.6 %collective-permute-start.40 = (bf16[64,2048]{0,1:T(8,128)(2,1)}, bf16[64,2048]{0,1:T(8,128)(2,1)}, u32[]{:S(2)}, u32[]{:S(2)}) collective-permute-start(bf16[64,2048]{0,1:T(8,128)(2,1)} %pad_maximum_fusion.6), channel_id=1, source_target_pairs={{0,16},{4,20},{8,24},{12,28},{16,0},{20,4},{24,8},{28,12},{1,17},{... | collective-permute-start | bytes 786440 | tf_op jit(solution)/shard_map/ppermute | solution.py:31
  600.2 38.5 %collective-permute-start.56 = (bf16[256,1024]{1,0:T(8,128)(2,1)}, bf16[256,1024]{1,0:T(8,128)(2,1)}, u32[]{:S(2)}, u32[]{:S(2)}) collective-permute-start(bf16[256,1024]{1,0:T(8,128)(2,1)} %pad_maximum_fusion.5), channel_id=1, source_target_pairs={{0,4},{4,0},{8,12},{12,8},{16,20},{20,16},{24,28},{28,24},{1,5},{5... | collective-permute-start | bytes 1572872 | tf_op jit(solution)/shard_map/ppermute | solution.py:31
  603.2 41.8 %collective-permute-start.34 = (bf16[2,256,1152]{1,2,0:T(8,128)(2,1)}, bf16[2,256,1152]{1,2,0:T(8,128)(2,1)}, u32[]{:S(2)}, u32[]{:S(2)}) collective-permute-start(bf16[2,256,1152]{1,2,0:T(8,128)(2,1)} %bitcast.509), channel_id=1, source_target_pairs={{0,1},{1,0},{2,3},{3,2},{4,5},{5,4},{6,7},{7,6},{8,9},{9,8},{10,11... | collective-permute-start | bytes 3538952 | tf_op jit(solution)/shard_map/ppermute | solution.py:31
  629.0 14.2 %collective-permute-start.41 = (bf16[128,2048]{0,1:T(8,128)(2,1)}, bf16[128,2048]{0,1:T(8,128)(2,1)}, u32[]{:S(2)}, u32[]{:S(2)}) collective-permute-start(bf16[128,2048]{0,1:T(8,128)(2,1)} %pad_maximum_fusion.7), channel_id=1, source_target_pairs={{0,8},{4,12},{8,0},{12,4},{16,24},{20,28},{24,16},{28,20},{1,9},{5... | collective-permute-start | bytes 1572872 | tf_op jit(solution)/shard_map/ppermute | solution.py:31
  638.6 9.4 %collective-permute-start.33 = (bf16[2,256,1152]{1,2,0:T(8,128)(2,1)}, bf16[2,256,1152]{1,2,0:T(8,128)(2,1)S(1)}, u32[]{:S(2)}, u32[]{:S(2)}) collective-permute-start(bf16[2,256,1152]{1,2,0:T(8,128)(2,1)} %bitcast.510), channel_id=1, source_target_pairs={{0,1},{1,0},{2,3},{3,2},{4,5},{5,4},{6,7},{7,6},{8,9},{9,8},{10,11... | collective-permute-start | bytes 3538952 | tf_op jit(solution)/shard_map/ppermute | solution.py:31
  659.0 1.6 collective-permute-start.35
  660.7 4.2 collective-permute-start.36
  665.0 4.2 collective-permute-start.37
  669.2 4.2 collective-permute-start.38
  671.0 16.6 %collective-permute-start.49 = (bf16[1,256,1152]{1,2,0:T(8,128)(2,1)}, bf16[1,256,1152]{1,2,0:T(8,128)(2,1)}, u32[]{:S(2)}, u32[]{:S(2)}) collective-permute-start(bf16[1,256,1152]{1,2,0:T(8,128)(2,1)} %dynamic-slice_convert_fusion.2), channel_id=1, source_target_pairs={{0,2},{1,3},{2,0},{3,1},{4,6},{5,7},{6,4},{7,5},{8,10},{9,11},{10,... | collective-permute-start | bytes 1769480 | tf_op jit(solution)/shard_map/ppermute | solution.py:31
  671.0 26.1 %collective-permute-start.42 = (bf16[1,256,1152]{1,2,0:T(8,128)(2,1)S(1)}, bf16[1,256,1152]{1,2,0:T(8,128)(2,1)}, u32[]{:S(2)}, u32[]{:S(2)}) collective-permute-start(bf16[1,256,1152]{1,2,0:T(8,128)(2,1)S(1)} %dynamic-slice_convert_fusion.3), channel_id=1, source_target_pairs={{0,2},{1,3},{2,0},{3,1},{4,6},{5,7},{6,4},{7,5},{8,10},{9,11},{10,... | collective-permute-start | bytes 1769480 | tf_op jit(solution)/shard_map/ppermute | solution.py:31
  673.3 5.0 collective-permute-start.39
  689.2 10.2 %collective-permute-start.50 = (bf16[128,1152]{0,1:T(8,128)(2,1)S(1)}, bf16[128,1152]{0,1:T(8,128)(2,1)S(1)}, u32[]{:S(2)}, u32[]{:S(2)}) collective-permute-start(bf16[128,1152]{0,1:T(8,128)(2,1)S(1)} %fusion.49), channel_id=1, source_target_pairs={{0,8},{4,12},{8,0},{12,4},{16,24},{20,28},{24,16},{28,20},{1,9},{5... | collective-permute-start | bytes 884744 | tf_op jit(solution)/shard_map/ppermute | solution.py:31
  698.3 6.8 collective-permute-start.43
  699.6 12.5 %collective-permute-start.51 = (bf16[64,1152]{0,1:T(8,128)(2,1)S(1)}, bf16[64,1152]{0,1:T(8,128)(2,1)S(1)}, u32[]{:S(2)}, u32[]{:S(2)}) collective-permute-start(bf16[64,1152]{0,1:T(8,128)(2,1)S(1)} %dynamic-slice_convert_fusion.9), channel_id=1, source_target_pairs={{0,16},{4,20},{8,24},{12,28},{16,0},{20,4},{24,8},{28,12},{1,17},{... | collective-permute-start | bytes 442376 | tf_op jit(solution)/shard_map/ppermute | solution.py:31
  705.3 9.8 %collective-permute-start.44 = (bf16[64,1152]{0,1:T(8,128)(2,1)S(1)}, bf16[64,1152]{0,1:T(8,128)(2,1)S(1)}, u32[]{:S(2)}, u32[]{:S(2)}) collective-permute-start(bf16[64,1152]{0,1:T(8,128)(2,1)S(1)} %dynamic-slice_convert_fusion.12), channel_id=1, source_target_pairs={{0,8},{4,12},{8,0},{12,4},{16,24},{20,28},{24,16},{28,20},{1,9},{5... | collective-permute-start | bytes 442376 | tf_op jit(solution)/shard_map/ppermute | solution.py:31
  712.6 7.1 collective-permute-start.52
  715.5 12.9 %collective-permute-start.45 = (bf16[32,1152]{0,1:T(8,128)(2,1)S(1)}, bf16[32,1152]{0,1:T(8,128)(2,1)S(1)}, u32[]{:S(2)}, u32[]{:S(2)}) collective-permute-start(bf16[32,1152]{0,1:T(8,128)(2,1)S(1)} %dynamic-slice_convert_fusion.11), channel_id=1, source_target_pairs={{0,16},{4,20},{8,24},{12,28},{16,0},{20,4},{24,8},{28,12},{1,17},{... | collective-permute-start | bytes 221192 | tf_op jit(solution)/shard_map/ppermute | solution.py:31
  719.9 8.9 %collective-permute-start.53 = (bf16[32,1152]{0,1:T(8,128)(2,1)S(1)}, bf16[32,1152]{0,1:T(8,128)(2,1)S(1)}, u32[]{:S(2)}, u32[]{:S(2)}) collective-permute-start(bf16[32,1152]{0,1:T(8,128)(2,1)S(1)} %add_convert_fusion.2), channel_id=1, source_target_pairs={{0,4},{4,0},{8,12},{12,8},{16,20},{20,16},{24,28},{28,24},{1,5},{5... | collective-permute-start | bytes 221192 | tf_op jit(solution)/shard_map/ppermute | solution.py:31
  728.7 22.3 %collective-permute-start.46 = (bf16[32,1152]{0,1:T(8,128)(2,1)S(1)}, bf16[32,1152]{0,1:T(8,128)(2,1)S(1)}, u32[]{:S(2)}, u32[]{:S(2)}) collective-permute-start(bf16[32,1152]{0,1:T(8,128)(2,1)S(1)} %add_convert_fusion.3), channel_id=1, source_target_pairs={{0,16},{4,20},{8,24},{12,28},{16,0},{20,4},{24,8},{28,12},{1,17},{... | collective-permute-start | bytes 221192 | tf_op jit(solution)/shard_map/ppermute | solution.py:31
  729.0 28.3 %collective-permute-start.54 = (bf16[64,1152]{0,1:T(8,128)(2,1)S(1)}, bf16[64,1152]{0,1:T(8,128)(2,1)S(1)}, u32[]{:S(2)}, u32[]{:S(2)}) collective-permute-start(bf16[64,1152]{0,1:T(8,128)(2,1)S(1)} %pad_maximum_fusion.10), channel_id=1, source_target_pairs={{0,16},{4,20},{8,24},{12,28},{16,0},{20,4},{24,8},{28,12},{1,17},{... | collective-permute-start | bytes 442376 | tf_op jit(solution)/shard_map/ppermute | solution.py:31
  751.2 12.4 %collective-permute-start.47 = (bf16[64,1152]{0,1:T(8,128)(2,1)S(1)}, bf16[64,1152]{0,1:T(8,128)(2,1)S(1)}, u32[]{:S(2)}, u32[]{:S(2)}) collective-permute-start(bf16[64,1152]{0,1:T(8,128)(2,1)S(1)} %pad_maximum_fusion.8), channel_id=1, source_target_pairs={{0,8},{4,12},{8,0},{12,4},{16,24},{20,28},{24,16},{28,20},{1,9},{5... | collective-permute-start | bytes 442376 | tf_op jit(solution)/shard_map/ppermute | solution.py:31
  757.8 12.1 %collective-permute-start.55 = (bf16[128,1152]{0,1:T(8,128)(2,1)S(1)}, bf16[128,1152]{0,1:T(8,128)(2,1)S(1)}, u32[]{:S(2)}, u32[]{:S(2)}) collective-permute-start(bf16[128,1152]{0,1:T(8,128)(2,1)S(1)} %pad_maximum_fusion.11), channel_id=1, source_target_pairs={{0,8},{4,12},{8,0},{12,4},{16,24},{20,28},{24,16},{28,20},{1,9},{5... | collective-permute-start | bytes 884744 | tf_op jit(solution)/shard_map/ppermute | solution.py:31
  764.1 8.9 %collective-permute-start.48 = (bf16[128,1152]{0,1:T(8,128)(2,1)S(1)}, bf16[128,1152]{0,1:T(8,128)(2,1)S(1)}, u32[]{:S(2)}, u32[]{:S(2)}) collective-permute-start(bf16[128,1152]{0,1:T(8,128)(2,1)S(1)} %pad_maximum_fusion.9), channel_id=1, source_target_pairs={{0,4},{4,0},{8,12},{12,8},{16,20},{20,16},{24,28},{28,24},{1,5},{5... | collective-permute-start | bytes 884744 | tf_op jit(solution)/shard_map/ppermute | solution.py:31
  (157 other events, 1147.9 us)
